TPU v7x, 32 devices: a whole 2x2x4 slice. The times are simulated.
32 devices in a mesh: pipe: 4 (over y, core), dp: 8 (over z, x).
Axes of the slice: x: 2, y: 2, z: 4, core: 2. Of those that a mesh axis runs over, the one named last changes fastest.
Arguments:
- tokens_in: bfloat16 [35840, 256], P('dp'), may hold values from -6 to 6
- cotangent: bfloat16 [35840, 256], P('dp'), may hold values from -6 to 6
- valid_mask: int32 [128, 280], P('dp'), may hold values from 0 to 1, as said below
- orientation: int32 [128], P('dp'), may hold values from 0 to 1
- dilation: int32 [128, 2], P('dp'), may hold values from 1 to 2
- norm_gain: bfloat16 [4, 256], P('pipe'), may hold values from 0.25 to 1.75
- norm_bias: bfloat16 [4, 256], P('pipe'), may hold values from -1.5 to 1.5
- in_weight: bfloat16 [4, 256, 768], P('pipe'), may hold values from -0.375 to 0.375
- in_bias: bfloat16 [4, 768], P('pipe'), may hold values from -1.5 to 1.5
- out_bias: bfloat16 [4, 256], P('pipe'), may hold values from -1.5 to 1.5
- proj_weight: bfloat16 [2, 256, 256], replicated, may hold values from -1.5 to 1.5
- down_weight: bfloat16 [2, 768, 256], replicated, may hold values from -0.21875 to 0.21875
- position_bias: bfloat16 [2, 8, 169], replicated, may hold values from -4 to 4
Outputs:
- section_outputs: bfloat16 [4, 35840, 256], P('pipe', 'dp')
- section_input_grads: bfloat16 [4, 35840, 256], P('pipe', 'dp')
- grad_norm_gain: float32 [4, 256], P('pipe')
- grad_norm_bias: float32 [4, 256], P('pipe')
- grad_in_weight: float32 [4, 256, 768], P('pipe')
- grad_in_bias: float32 [4, 768], P('pipe')
- grad_out_bias: float32 [4, 256], P('pipe')
- grad_proj: float32 [2, 256, 256], replicated
- grad_down: float32 [2, 768, 256], replicated
- grad_position_bias: float32 [2, 8, 169], replicated
Inputs may be any that keep to these rules, and one draw needn't show every extreme that they name: `valid_mask`: each image's valid tokens are the grid rows 0 to r - 1 and columns 0 to c - 1, with 8 <= r <= 14 and 14 <= c <= 20.
All inputs are finite; a program needn't handle non-finite values.
Results may differ from a plain program's by a relative error of at most 0.017.
Values may be sent and summed in bfloat16 or wider, within the bound.
A program may use at most 448 MiB of HBM per device.

v0:
```python
import jax
import jax.numpy as jnp
from jax import lax
from jax.sharding import PartitionSpec as P

HEADS = 8
HEAD = 32
KS = 7
R_SIDE = 14
C_SIDE = 20
MICRO = 4
PIX = 280


EPS = 1e-05
NEG = -1e30
HIGH = lax.Precision.HIGHEST


def from_behind(block, axis, distance):
    devices = range(lax.axis_size(axis))
    route = [(i - distance, i) for i in devices if i - distance in devices]
    return lax.ppermute(block, axis, route)


def norm_rows(x, gain, shift):
    center = x - jnp.mean(x, axis=-1, keepdims=True)
    spread = jnp.mean(center * center, axis=-1, keepdims=True)
    return center * lax.rsqrt(spread + EPS) * gain + shift


def window_tables(spacing_in, length):
    places = jnp.arange(length, dtype=jnp.int32)
    spacing = spacing_in[:, None]
    group = places[None, :] % spacing
    local = places[None, :] // spacing
    count = (length - group + spacing - 1) // spacing
    start = jnp.clip(local - KS // 2, 0, count - KS)
    same = group[:, :, None] == group[:, None, :]
    reach = local[:, None, :] - start[:, :, None]
    inside = same & (reach >= 0) & (reach < KS)
    offset = local[:, None, :] - local[:, :, None] + KS - 1
    ladder = jnp.arange(2 * KS - 1, dtype=jnp.int32)
    onehot = (inside[..., None] & (offset[..., None] == ladder)).astype(jnp.bfloat16)
    return (inside, onehot)


def geometry(mask, turn, spacing):
    count = mask.shape[0]
    row_in, row_hot = window_tables(spacing, R_SIDE)
    col_in, col_hot = window_tables(spacing, C_SIDE)
    valid = mask.reshape(count, R_SIDE, C_SIDE) > 0
    allowed = row_in[:, :, None, :, None] & col_in[:, None, :, None, :] & valid[:, None, None, :, :]
    return (allowed.reshape(count, PIX, PIX), row_hot, col_hot, turn)


def head_bias(table, geo):
    allowed, row_hot, col_hot, turn = geo
    turned = jnp.where(turn[:, None, None] == 1, table.T[None], table[None])
    first = jnp.einsum(
        "nxua,nab->nxub", row_hot, turned, preferred_element_type=jnp.float32
    ).astype(jnp.bfloat16)
    full = jnp.einsum("nxub,nyvb->nxyuv", first, col_hot, preferred_element_type=jnp.float32)
    return full.reshape(allowed.shape)


def bias_term(dscore, geo):
    allowed, row_hot, col_hot, turn = geo
    count = dscore.shape[0]
    five = dscore.reshape(count, R_SIDE, C_SIDE, R_SIDE, C_SIDE)
    upper = five.astype(jnp.bfloat16)
    lower = (five - upper.astype(jnp.float32)).astype(jnp.bfloat16)
    first = jnp.einsum("nxyuv,nyvb->nxub", upper, col_hot, preferred_element_type=jnp.float32)
    first = first + jnp.einsum(
        "nxyuv,nyvb->nxub", lower, col_hot, preferred_element_type=jnp.float32
    )
    every = jnp.einsum("nxub,nxua->nab", first, row_hot.astype(jnp.float32), precision=HIGH)
    turned = jnp.where(turn[:, None, None] == 1, jnp.swapaxes(every, 1, 2), every)
    return jnp.sum(turned, axis=0)


def head_scores(query, keys, table, geo):
    raw = jnp.einsum("npe,nke->npk", query, keys, preferred_element_type=jnp.float32)
    return jnp.where(geo[0], raw + head_bias(table, geo), NEG)


def head_forward(query, keys, values, table, geo):
    scores = head_scores(query, keys, table, geo)
    top = jnp.max(scores, axis=-1, keepdims=True)
    expo = jnp.exp(scores - top)
    total = jnp.sum(expo, axis=-1, keepdims=True)
    weights = (expo / total).astype(jnp.bfloat16)
    result = jnp.einsum("npk,nke->npe", weights, values, preferred_element_type=jnp.float32)
    return (result, top + jnp.log(total))


def head_backward(query, keys, values, table, logsum, upstream, geo):
    scores = head_scores(query, keys, table, geo)
    weights = jnp.exp(scores - logsum)
    rounded = weights.astype(jnp.bfloat16)
    dweight = jnp.einsum("npe,nke->npk", upstream, values, preferred_element_type=jnp.float32)
    dscore = weights * (dweight - jnp.sum(weights * dweight, axis=-1, keepdims=True))
    table_grad = bias_term(dscore, geo)
    dscore_low = dscore.astype(jnp.bfloat16)
    dquery = jnp.einsum("npk,nke->npe", dscore_low, keys, preferred_element_type=jnp.float32)
    dkeys = jnp.einsum("npk,npe->nke", dscore_low, query, preferred_element_type=jnp.float32)
    dvalues = jnp.einsum("npk,npe->nke", rounded, upstream, preferred_element_type=jnp.float32)
    return (dquery, dkeys, dvalues, table_grad)


def split_heads(matrix, count):
    return matrix.reshape(count, PIX, HEADS, HEAD).transpose(2, 0, 1, 3)


def merge_heads(stack):
    return stack.transpose(1, 2, 0, 3).reshape(
        stack.shape[1] * stack.shape[2], stack.shape[0] * stack.shape[3]
    )


def attention_inner(xb, gain, shift, w_in, b_in, tables, geo):
    x = xb.astype(jnp.float32)
    width = x.shape[1]
    count = geo[0].shape[0]
    normed_full, norm_back = jax.vjp(
        norm_rows, x, gain.astype(jnp.float32), shift.astype(jnp.float32)
    )
    normed = normed_full.astype(jnp.bfloat16)
    mixed = jnp.dot(normed, w_in, preferred_element_type=jnp.float32) + b_in
    query = split_heads((mixed[:, :width] * HEAD ** (-0.5)).astype(jnp.bfloat16), count)
    keys = split_heads(mixed[:, width : 2 * width].astype(jnp.bfloat16), count)
    values = split_heads(mixed[:, 2 * width :].astype(jnp.bfloat16), count)

    def one_head(q_part, k_part, v_part, t_part):
        return head_forward(q_part, k_part, v_part, t_part, geo)

    heads, logsum = jax.vmap(one_head)(query, keys, values, tables)
    attended = merge_heads(heads).astype(jnp.bfloat16)
    return (x, normed, norm_back, query, keys, values, logsum, attended)


def attention_forward(xb, gain, shift, w_in, b_in, w_proj, b_out, tables, geo):
    x, normed, norm_back, query, keys, values, logsum, attended = attention_inner(
        xb, gain, shift, w_in, b_in, tables, geo
    )
    return x + jnp.dot(attended, w_proj, preferred_element_type=jnp.float32) + b_out


def attention_backward(xb, upstream, gain, shift, w_in, b_in, w_proj, tables, geo):
    x, normed, norm_back, query, keys, values, logsum, attended = attention_inner(
        xb, gain, shift, w_in, b_in, tables, geo
    )
    count = geo[0].shape[0]
    flow = upstream.astype(jnp.float32)
    outer_bias = jnp.sum(flow, axis=0)
    mixer_term = jnp.einsum("nd,ne->de", attended, upstream, preferred_element_type=jnp.float32)
    dattended = jnp.einsum(
        "ne,de->nd", upstream, w_proj, preferred_element_type=jnp.float32
    ).astype(jnp.bfloat16)

    def one_head(q_part, k_part, v_part, t_part, l_part, u_part):
        return head_backward(q_part, k_part, v_part, t_part, l_part, u_part, geo)

    dquery, dkeys, dvalues, table_grad = jax.vmap(one_head)(
        query, keys, values, tables, logsum, split_heads(dattended, count)
    )
    dmixed = jnp.concatenate(
        [merge_heads(dquery) * HEAD ** (-0.5), merge_heads(dkeys), merge_heads(dvalues)], axis=1
    ).astype(jnp.bfloat16)
    inner_term = jnp.einsum("nd,nf->df", normed, dmixed, preferred_element_type=jnp.float32)
    inner_bias = jnp.sum(dmixed, axis=0, dtype=jnp.float32)
    dnormed = jnp.einsum("nf,df->nd", dmixed, w_in, preferred_element_type=jnp.float32)
    dinput, gain_term, shift_term = norm_back(dnormed)
    return (
        flow + dinput,
        gain_term,
        shift_term,
        inner_term,
        inner_bias,
        outer_bias,
        mixer_term,
        table_grad,
    )


def exact_gelu(value):
    return jax.nn.gelu(value, approximate=False)


def mlp_inner(xb, gain, shift, w_in, b_in):
    x = xb.astype(jnp.float32)
    normed_full, norm_back = jax.vjp(
        norm_rows, x, gain.astype(jnp.float32), shift.astype(jnp.float32)
    )
    normed = normed_full.astype(jnp.bfloat16)
    hidden = jnp.dot(normed, w_in, preferred_element_type=jnp.float32) + b_in
    active_full, gelu_back = jax.vjp(exact_gelu, hidden)
    return (x, normed, norm_back, active_full.astype(jnp.bfloat16), gelu_back)


def mlp_forward(xb, gain, shift, w_in, b_in, w_down, b_out):
    x, normed, norm_back, active, gelu_back = mlp_inner(xb, gain, shift, w_in, b_in)
    return x + jnp.dot(active, w_down, preferred_element_type=jnp.float32) + b_out


def mlp_backward(xb, upstream, gain, shift, w_in, b_in, w_down):
    x, normed, norm_back, active, gelu_back = mlp_inner(xb, gain, shift, w_in, b_in)
    flow = upstream.astype(jnp.float32)
    outer_bias = jnp.sum(flow, axis=0)
    down_term = jnp.einsum("nf,nd->fd", active, upstream, preferred_element_type=jnp.float32)
    spread = jnp.einsum("nd,fd->nf", upstream, w_down, preferred_element_type=jnp.float32)
    dhidden = gelu_back(spread)[0].astype(jnp.bfloat16)
    inner_term = jnp.einsum("nd,nf->df", normed, dhidden, preferred_element_type=jnp.float32)
    inner_bias = jnp.sum(dhidden, axis=0, dtype=jnp.float32)
    dnormed = jnp.einsum("nf,df->nd", dhidden, w_in, preferred_element_type=jnp.float32)
    dinput, gain_term, shift_term = norm_back(dnormed)
    return (flow + dinput, gain_term, shift_term, inner_term, inner_bias, outer_bias, down_term)


def combine(section_terms, block_terms):
    section_sums = lax.psum(
        (section_terms[0], section_terms[1], section_terms[2], section_terms[3], section_terms[4]),
        "dp",
    )
    block_sums = lax.psum((block_terms[0], block_terms[1], block_terms[2]), ("pipe", "dp"))
    return tuple(section_sums) + tuple(block_sums)


def body(
    tokens_in,
    cotangent,
    valid_mask,
    orientation,
    dilation,
    norm_gain,
    norm_bias,
    in_weight,
    in_bias,
    out_bias,
    proj_weight,
    down_weight,
    position_bias,
):
    width = tokens_in.shape[1]
    hidden_width = in_weight.shape[2]
    blocks = proj_weight.shape[0]
    rows_micro = tokens_in.shape[0] // MICRO
    images_micro = valid_mask.shape[0] // MICRO
    span = 2 * KS - 1
    tables = position_bias.reshape(blocks, HEADS, span, span)
    sections_count = lax.axis_size("pipe")

    def micro_rows(source, index):
        return lax.dynamic_slice_in_dim(source, index * rows_micro, rows_micro, 0)

    def micro_geometry(index, block):
        mask = lax.dynamic_slice_in_dim(valid_mask, index * images_micro, images_micro, 0)
        turn = lax.dynamic_slice_in_dim(orientation, index * images_micro, images_micro, 0)
        spacing = lax.dynamic_slice_in_dim(dilation, index * images_micro, images_micro, 0)
        return geometry(mask, turn, jnp.take(spacing, block, axis=1))

    section = lax.axis_index("pipe")
    last = sections_count - 1
    block = section // 2
    is_attention = section % 2 == 0
    gain = norm_gain[0]
    shift = norm_bias[0]
    w_in = in_weight[0]
    b_in = in_bias[0]
    b_out = out_bias[0]
    w_proj = proj_weight[block]
    w_down = down_weight[block]
    own_tables = tables[block]

    def forward_at(xb, index):
        return lax.cond(
            is_attention,
            lambda: attention_forward(
                xb, gain, shift, w_in, b_in, w_proj, b_out, own_tables, micro_geometry(index, block)
            ),
            lambda: mlp_forward(xb, gain, shift, w_in, b_in, w_down, b_out),
        )

    def backward_at(xb, upstream, index):

        def attention_side():
            result = attention_backward(
                xb,
                upstream,
                gain,
                shift,
                w_in,
                b_in,
                w_proj,
                own_tables,
                micro_geometry(index, block),
            )
            return result[:7] + (jnp.zeros((hidden_width, width), jnp.float32), result[7])

        def mlp_side():
            result = mlp_backward(xb, upstream, gain, shift, w_in, b_in, w_down)
            return result[:6] + (
                jnp.zeros((width, width), jnp.float32),
                result[6],
                jnp.zeros((HEADS, span, span), jnp.float32),
            )

        return lax.cond(is_attention, attention_side, mlp_side)

    empty_rows = jnp.zeros((rows_micro, width), jnp.bfloat16)
    inbound = empty_rows
    kept = jnp.zeros((MICRO, rows_micro, width), jnp.bfloat16)
    results = jnp.zeros((MICRO, rows_micro, width), jnp.bfloat16)
    for tick in range(MICRO + sections_count - 1):
        index = tick - section
        live = (index >= 0) & (index < MICRO)
        safe = jnp.clip(index, 0, MICRO - 1)
        xb = jnp.where(section == 0, micro_rows(tokens_in, safe), inbound)
        output = lax.cond(
            live, lambda: forward_at(xb, safe), lambda: jnp.zeros((rows_micro, width), jnp.float32)
        )
        output_low = output.astype(jnp.bfloat16)
        kept = lax.dynamic_update_index_in_dim(kept, jnp.where(live, xb, kept[safe]), safe, 0)
        results = lax.dynamic_update_index_in_dim(
            results, jnp.where(live, output_low, results[safe]), safe, 0
        )
        if tick < MICRO + sections_count - 2:
            inbound = from_behind(output_low, "pipe", 1)
    blank = (
        jnp.zeros((rows_micro, width), jnp.float32),
        jnp.zeros((width,), jnp.float32),
        jnp.zeros((width,), jnp.float32),
        jnp.zeros((width, hidden_width), jnp.float32),
        jnp.zeros((hidden_width,), jnp.float32),
        jnp.zeros((width,), jnp.float32),
        jnp.zeros((width, width), jnp.float32),
        jnp.zeros((hidden_width, width), jnp.float32),
        jnp.zeros((HEADS, span, span), jnp.float32),
    )
    totals = blank[1:]
    inbound = empty_rows
    backs = jnp.zeros((MICRO, rows_micro, width), jnp.bfloat16)
    for tick in range(MICRO + sections_count - 1):
        index = tick - (last - section)
        live = (index >= 0) & (index < MICRO)
        safe = jnp.clip(index, 0, MICRO - 1)
        upstream = jnp.where(section == last, micro_rows(cotangent, safe), inbound)
        outcome = lax.cond(live, lambda: backward_at(kept[safe], upstream, safe), lambda: blank)
        totals = tuple((a + b for a, b in zip(totals, outcome[1:])))
        back_low = outcome[0].astype(jnp.bfloat16)
        backs = lax.dynamic_update_index_in_dim(
            backs, jnp.where(live, back_low, backs[safe]), safe, 0
        )
        if tick < MICRO + sections_count - 2:
            inbound = from_behind(back_low, "pipe", -1)
    section_out = results.reshape(1, MICRO * rows_micro, width)
    section_back = backs.reshape(1, MICRO * rows_micro, width)
    section_terms = tuple((term[None] for term in totals[:5]))
    mixer_terms = lax.dynamic_update_index_in_dim(
        jnp.zeros((blocks, width, width), jnp.float32), totals[5], block, 0
    )
    down_terms = lax.dynamic_update_index_in_dim(
        jnp.zeros((blocks, hidden_width, width), jnp.float32), totals[6], block, 0
    )
    table_terms = lax.dynamic_update_index_in_dim(
        jnp.zeros((blocks, HEADS, span * span), jnp.float32),
        totals[7].reshape(HEADS, span * span),
        block,
        0,
    )
    finals = combine(section_terms, (mixer_terms, down_terms, table_terms))
    return (section_out, section_back) + finals


def solution(mesh):
    placed = (
        P("dp", None),
        P("dp", None),
        P("dp", None),
        P("dp"),
        P("dp", None),
        P("pipe", None),
        P("pipe", None),
        P("pipe", None, None),
        P("pipe", None),
        P("pipe", None),
        P(),
        P(),
        P(),
    )
    return jax.shard_map(
        body,
        mesh=mesh,
        in_specs=placed,
        out_specs=(
            P("pipe", "dp", None),
            P("pipe", "dp", None),
            P("pipe", None),
            P("pipe", None),
            P("pipe", None, None),
            P("pipe", None),
            P("pipe", None),
            P(),
            P(),
            P(),
        ),
        check_vma=False,
    )
```

profile of v0, /device:TPU:1, one launch (start us, length us, event | category | flops | bytes accessed | tf_op | source)
XLA Modules:
  0.0 4397.0 jit_solution(6005186722739616452)
XLA Ops:
  32.8 224.1 %collective-permute-done = bf16[1120,256]{1,0:T(8,128)(2,1)} collective-permute-done((bf16[1120,256]{1,0:T(8,128)(2,1)}, bf16[1120,256]{1,0:T(8,128)(2,1)}, u32[]{:S(2)}, u32[]{:S(2)}) %collective-permute-start) | collective-permute-done | bytes 573472 | tf_op jit(solution)/shard_map/ppermute | solution.py:23
  259.2 19.7 conditional.85
  259.2 12.0 conditional.27
  286.0 215.9 %collective-permute-done.1 = bf16[1120,256]{1,0:T(8,128)(2,1)S(1)} collective-permute-done((bf16[1120,256]{1,0:T(8,128)(2,1)}, bf16[1120,256]{1,0:T(8,128)(2,1)S(1)}, u32[]{:S(2)}, u32[]{:S(2)}) %collective-permute-start.1) | collective-permute-done | bytes 573472 | tf_op jit(solution)/shard_map/ppermute | solution.py:23
  504.0 19.9 conditional.86
  504.0 12.3 conditional.28
  536.3 211.2 %collective-permute-done.2 = bf16[1120,256]{1,0:T(8,128)(2,1)S(1)} collective-permute-done((bf16[1120,256]{1,0:T(8,128)(2,1)}, bf16[1120,256]{1,0:T(8,128)(2,1)S(1)}, u32[]{:S(2)}, u32[]{:S(2)}) %collective-permute-start.2) | collective-permute-done | bytes 573472 | tf_op jit(solution)/shard_map/ppermute | solution.py:23
  749.7 21.1 conditional.87
  749.7 18.9 conditional.29
  781.3 206.4 %collective-permute-done.3 = bf16[1120,256]{1,0:T(8,128)(2,1)S(1)} collective-permute-done((bf16[1120,256]{1,0:T(8,128)(2,1)}, bf16[1120,256]{1,0:T(8,128)(2,1)S(1)}, u32[]{:S(2)}, u32[]{:S(2)}) %collective-permute-start.3) | collective-permute-done | bytes 573472 | tf_op jit(solution)/shard_map/ppermute | solution.py:23
  989.8 19.7 conditional.88
  989.8 12.0 conditional.36
  1009.5 17.0 collective-permute-start.4
  1047.0 232.7 %collective-permute-start.5 = (bf16[1120,256]{1,0:T(8,128)(2,1)}, bf16[1120,256]{1,0:T(8,128)(2,1)S(1)}, u32[]{:S(2)}, u32[]{:S(2)}) collective-permute-start(bf16[1120,256]{1,0:T(8,128)(2,1)} %get-tuple-element.4120), channel_id=1, source_target_pairs={{0,8},{8,16},{16,24},{1,9},{9,17},{17,25},{2,10},{10,18},{18,26},{... | collective-permute-start | bytes 1720328 | tf_op jit(solution)/shard_map/ppermute | solution.py:23
  1289.0 13.7 conditional.91
  1306.7 12.1 conditional.90
  1320.9 16.8 conditional.92
  1343.6 549.2 %collective-permute-done.7 = bf16[1120,256]{1,0:T(8,128)(2,1)S(1)} collective-permute-done((bf16[1120,256]{1,0:T(8,128)(2,1)}, bf16[1120,256]{1,0:T(8,128)(2,1)S(1)}, u32[]{:S(2)}, u32[]{:S(2)}) %collective-permute-start.7) | collective-permute-done | bytes 573472 | tf_op jit(solution)/shard_map/ppermute | solution.py:23
  1892.8 47.2 %conditional.93 = ((f32[256]{0:T(256)}, f32[256]{0:T(256)}, f32[256,768]{1,0:T(8,128)}, f32[768]{0:T(1024)}, f32[256]{0:T(256)}, /*index=5*/f32[256,256]{1,0:T(8...) conditional(s32[]{:T(128)} %convert_element_type.1444, () %tuple.411, ...), branch_computations={%region_118.126_spmd, %region_119.149_spmd} | conditional | flops 2864387328 | bytes 410919872 | solution.py:348
  1895.9 34.2 conditional.112
  1946.1 507.3 %collective-permute-done.8 = bf16[1120,256]{1,0:T(8,128)(2,1)S(1)} collective-permute-done((bf16[1120,256]{1,0:T(8,128)(2,1)}, bf16[1120,256]{1,0:T(8,128)(2,1)S(1)}, u32[]{:S(2)}, u32[]{:S(2)}) %collective-permute-start.8) | collective-permute-done | bytes 573472 | tf_op jit(solution)/shard_map/ppermute | solution.py:23
  2453.4 46.7 %conditional.94 = ((f32[256]{0:T(256)}, f32[256]{0:T(256)}, f32[256,768]{1,0:T(8,128)}, f32[768]{0:T(1024)}, f32[256]{0:T(256)}, /*index=5*/f32[256,256]{1,0:T(8...) conditional(s32[]{:T(128)} %convert_element_type.1445, () %tuple.413, ...), branch_computations={%region_142.150_spmd, %region_143.173_spmd} | conditional | flops 2864387328 | bytes 410919872 | solution.py:348
  2456.5 43.6 conditional.113
  2506.1 497.9 %collective-permute-done.9 = bf16[1120,256]{1,0:T(8,128)(2,1)S(1)} collective-permute-done((bf16[1120,256]{1,0:T(8,128)(2,1)}, bf16[1120,256]{1,0:T(8,128)(2,1)S(1)}, u32[]{:S(2)}, u32[]{:S(2)}) %collective-permute-start.9) | collective-permute-done | bytes 573472 | tf_op jit(solution)/shard_map/ppermute | solution.py:23
  3004.0 55.9 %conditional.95 = ((f32[256]{0:T(256)}, f32[256]{0:T(256)}, f32[256,768]{1,0:T(8,128)}, f32[768]{0:T(1024)}, f32[256]{0:T(256)}, /*index=5*/f32[256,256]{1,0:T(8...) conditional(s32[]{:T(128)} %convert_element_type.1446, () %tuple.415, ...), branch_computations={%region_166.174_spmd, %region_167.197_spmd} | conditional | flops 2864387328 | bytes 410919872 | solution.py:348
  3007.1 42.8 conditional.114
  3066.0 498.6 %collective-permute-done.10 = bf16[1120,256]{1,0:T(8,128)(2,1)S(1)} collective-permute-done((bf16[1120,256]{1,0:T(8,128)(2,1)}, bf16[1120,256]{1,0:T(8,128)(2,1)S(1)}, u32[]{:S(2)}, u32[]{:S(2)}) %collective-permute-start.10) | collective-permute-done | bytes 573472 | tf_op jit(solution)/shard_map/ppermute | solution.py:23
  3564.7 47.5 %conditional.108 = ((f32[256]{0:T(256)}, f32[256]{0:T(256)}, f32[256,768]{1,0:T(8,128)}, f32[768]{0:T(1024)}, f32[256]{0:T(256)}, /*index=5*/f32[256,256]{1,0:T(...) conditional(s32[]{:T(128)} %convert_element_type.1447, () %tuple.417, ...), branch_computations={%region_190.198_spmd, %region_191.221_spmd} | conditional | flops 2864387328 | bytes 410919872 | solution.py:348
  3567.8 34.3 conditional.115
  3646.3 20.1 all-reduce.1
  3666.4 572.7 %psum.63 = f32[2,8,169]{2,1,0:T(8,128)} all-reduce(f32[2,8,169]{2,1,0:T(8,128)S(1)} %constant_dynamic-update-slice_fusion.21), channel_id=1, replica_groups=mesh['pipe'=4,'dp'=8] {'pipe','dp'}, use_global_device_ids=true, to_apply=%region_245.253 | all-reduce | flops 2704 | bytes 21632 | tf_op jit(solution)/shard_map/psum | solution.py:225
  4243.9 140.5 %all-reduce.7.cloned.1.call-done = (f32[2,256,256]{2,1,0:T(8,128)}, f32[2,768,256]{2,1,0:T(8,128)}) async-done(((f32[2,256,256]{2,1,0:T(8,128)}, f32[2,768,256]{2,1,0:T(8,128)}), (f32[2,256,256]{2,1,0:T(8,128)}, f32[2,768,256]{2,1,0:T(8,128)})) %all-reduce.7.cloned.1.call-update) | async-done | bytes 2097168 | tf_op jit(solution)/shard_map/psum | solution.py:225
  (308 shorter events, 357.5 us)
Async XLA Ops:
  7.2 3.9 copy-start
  7.2 9.2 copy-start.11
  7.2 9.2 copy-start.167
  7.2 9.2 copy-start.110
  7.2 9.2 copy-start.196
  7.2 4236.6 %all-reduce.5.cloned.1.call-start = ((), (), s32[]{:S(2)}) async-start(), calls=%async_computation | async-start | bytes 1572864 | tf_op jit(solution)/shard_map/psum | solution.py:221
  8.1 1027.5 %copy-start.183 = (bf16[256]{0:T(256)(128)(2,1)}, bf16[256]{0:T(256)(128)(2,1)S(1)}, u32[]{:S(2)}) copy-start(bf16[256]{0:T(256)(128)(2,1)S(1)} %reduce) | copy-start | bytes 1540
  8.8 1026.8 %copy-start.185 = (bf16[256]{0:T(256)(128)(2,1)}, bf16[256]{0:T(256)(128)(2,1)S(1)}, u32[]{:S(2)}) copy-start(bf16[256]{0:T(256)(128)(2,1)S(1)} %reduce.1) | copy-start | bytes 1540
  9.5 1026.1 %copy-start.100 = (bf16[768]{0:T(1024)(128)(2,1)}, bf16[768]{0:T(1024)(128)(2,1)S(1)}, u32[]{:S(2)}) copy-start(bf16[768]{0:T(1024)(128)(2,1)S(1)} %reduce.2) | copy-start | bytes 4612
  10.2 1025.4 %copy-start.194 = (bf16[256]{0:T(256)(128)(2,1)}, bf16[256]{0:T(256)(128)(2,1)S(1)}, u32[]{:S(2)}) copy-start(bf16[256]{0:T(256)(128)(2,1)S(1)} %reduce.3) | copy-start | bytes 1540
  11.9 1023.7 %copy-start.9 = (bf16[1,8,13,13]{3,2,1,0:T(8,128)(2,1)}, bf16[1,8,13,13]{3,2,1,0:T(8,128)(2,1)S(1)}, u32[]{:S(2)}) copy-start(bf16[1,8,13,13]{3,2,1,0:T(8,128)(2,1)S(1)} %constant_dynamic-slice_fusion.18) | copy-start | bytes 8116
  11.9 1023.7 %copy-start.68 = (bf16[1,8,13,13]{3,1,2,0:T(8,128)(2,1)}, bf16[1,8,13,13]{3,1,2,0:T(8,128)(2,1)S(1)}, u32[]{:S(2)}) copy-start(bf16[1,8,13,13]{3,1,2,0:T(8,128)(2,1)S(1)} %copy.1033) | copy-start | bytes 8116
  12.8 1022.8 %copy-start.41 = (bf16[256,256]{1,0:T(8,128)(2,1)}, bf16[256,256]{1,0:T(8,128)(2,1)S(1)}, u32[]{:S(2)}) copy-start(bf16[256,256]{1,0:T(8,128)(2,1)S(1)} %dynamic-slice_bitcast_fusion.8) | copy-start | bytes 393220
  25.3 231.5 %collective-permute-start = (bf16[1120,256]{1,0:T(8,128)(2,1)}, bf16[1120,256]{1,0:T(8,128)(2,1)}, u32[]{:S(2)}, u32[]{:S(2)}) collective-permute-start(bf16[1120,256]{1,0:T(8,128)(2,1)} %get-tuple-element.4115), channel_id=1, source_target_pairs={{0,8},{8,16},{16,24},{1,9},{9,17},{17,25},{2,10},{10,18},{18,26},{... | collective-permute-start | bytes 1720328 | tf_op jit(solution)/shard_map/ppermute | solution.py:23
  278.9 223.0 %collective-permute-start.1 = (bf16[1120,256]{1,0:T(8,128)(2,1)}, bf16[1120,256]{1,0:T(8,128)(2,1)S(1)}, u32[]{:S(2)}, u32[]{:S(2)}) collective-permute-start(bf16[1120,256]{1,0:T(8,128)(2,1)} %get-tuple-element.4116), channel_id=1, source_target_pairs={{0,8},{8,16},{16,24},{1,9},{9,17},{17,25},{2,10},{10,18},{18,26},{... | collective-permute-start | bytes 1720328 | tf_op jit(solution)/shard_map/ppermute | solution.py:23
  523.9 223.6 %collective-permute-start.2 = (bf16[1120,256]{1,0:T(8,128)(2,1)}, bf16[1120,256]{1,0:T(8,128)(2,1)S(1)}, u32[]{:S(2)}, u32[]{:S(2)}) collective-permute-start(bf16[1120,256]{1,0:T(8,128)(2,1)} %get-tuple-element.4117), channel_id=1, source_target_pairs={{0,8},{8,16},{16,24},{1,9},{9,17},{17,25},{2,10},{10,18},{18,26},{... | collective-permute-start | bytes 1720328 | tf_op jit(solution)/shard_map/ppermute | solution.py:23
  770.8 216.9 %collective-permute-start.3 = (bf16[1120,256]{1,0:T(8,128)(2,1)}, bf16[1120,256]{1,0:T(8,128)(2,1)S(1)}, u32[]{:S(2)}, u32[]{:S(2)}) collective-permute-start(bf16[1120,256]{1,0:T(8,128)(2,1)} %get-tuple-element.4118), channel_id=1, source_target_pairs={{0,8},{8,16},{16,24},{1,9},{9,17},{17,25},{2,10},{10,18},{18,26},{... | collective-permute-start | bytes 1720328 | tf_op jit(solution)/shard_map/ppermute | solution.py:23
  1009.5 23.9 collective-permute-start.4
  1047.0 239.6 %collective-permute-start.5 = (bf16[1120,256]{1,0:T(8,128)(2,1)}, bf16[1120,256]{1,0:T(8,128)(2,1)S(1)}, u32[]{:S(2)}, u32[]{:S(2)}) collective-permute-start(bf16[1120,256]{1,0:T(8,128)(2,1)} %get-tuple-element.4120), channel_id=1, source_target_pairs={{0,8},{8,16},{16,24},{1,9},{9,17},{17,25},{2,10},{10,18},{18,26},{... | collective-permute-start | bytes 1720328 | tf_op jit(solution)/shard_map/ppermute | solution.py:23
  1302.8 18.1 collective-permute-start.6
  1337.7 555.1 %collective-permute-start.7 = (bf16[1120,256]{1,0:T(8,128)(2,1)}, bf16[1120,256]{1,0:T(8,128)(2,1)S(1)}, u32[]{:S(2)}, u32[]{:S(2)}) collective-permute-start(bf16[1120,256]{1,0:T(8,128)(2,1)} %get-tuple-element.2937), channel_id=1, source_target_pairs={{8,0},{16,8},{24,16},{9,1},{17,9},{25,17},{10,2},{18,10},{26,18},{... | collective-permute-start | bytes 1720328 | tf_op jit(solution)/shard_map/ppermute | solution.py:23
  1907.1 3.6 copy-start.17
  1940.0 513.3 %collective-permute-start.8 = (bf16[1120,256]{1,0:T(8,128)(2,1)}, bf16[1120,256]{1,0:T(8,128)(2,1)S(1)}, u32[]{:S(2)}, u32[]{:S(2)}) collective-permute-start(bf16[1120,256]{1,0:T(8,128)(2,1)} %get-tuple-element.2938), channel_id=1, source_target_pairs={{8,0},{16,8},{24,16},{9,1},{17,9},{25,17},{10,2},{18,10},{26,18},{... | collective-permute-start | bytes 1720328 | tf_op jit(solution)/shard_map/ppermute | solution.py:23
  2467.7 3.6 copy-start.19
  2500.1 503.9 %collective-permute-start.9 = (bf16[1120,256]{1,0:T(8,128)(2,1)}, bf16[1120,256]{1,0:T(8,128)(2,1)S(1)}, u32[]{:S(2)}, u32[]{:S(2)}) collective-permute-start(bf16[1120,256]{1,0:T(8,128)(2,1)} %get-tuple-element.2939), channel_id=1, source_target_pairs={{8,0},{16,8},{24,16},{9,1},{17,9},{25,17},{10,2},{18,10},{26,18},{... | collective-permute-start | bytes 1720328 | tf_op jit(solution)/shard_map/ppermute | solution.py:23
  3060.0 504.7 %collective-permute-start.10 = (bf16[1120,256]{1,0:T(8,128)(2,1)}, bf16[1120,256]{1,0:T(8,128)(2,1)S(1)}, u32[]{:S(2)}, u32[]{:S(2)}) collective-permute-start(bf16[1120,256]{1,0:T(8,128)(2,1)} %get-tuple-element.2940), channel_id=1, source_target_pairs={{8,0},{16,8},{24,16},{9,1},{17,9},{25,17},{10,2},{18,10},{26,18},{... | collective-permute-start | bytes 1720328 | tf_op jit(solution)/shard_map/ppermute | solution.py:23
  3578.9 3.6 copy-start.23
  3612.2 11.2 collective-permute-start.11
  3636.9 747.5 %all-reduce.7.cloned.1.call-start = ((), (), s32[]{:S(2)}) async-start(), calls=%async_computation.1 | async-start | bytes 4194304 | tf_op jit(solution)/shard_map/psum | solution.py:225
  3639.9 599.3 %copy-start.91 = (bf16[1,1120,256]{2,1,0:T(8,128)(2,1)S(1)}, bf16[1,1120,256]{2,1,0:T(8,128)(2,1)}, u32[]{:S(2)}) copy-start(bf16[1,1120,256]{2,1,0:T(8,128)(2,1)} %constant_dynamic-slice_fusion) | copy-start | bytes 1720324
  4239.1 150.5 %copy-start.1 = (bf16[2,768,256]{2,1,0:T(8,128)(2,1)S(1)}, bf16[2,768,256]{2,1,0:T(8,128)(2,1)}, u32[]{:S(2)}) copy-start(bf16[2,768,256]{2,1,0:T(8,128)(2,1)} %param.94) | copy-start | bytes 2359300
  4384.4 4.1 copy-start.109
  (16 other events, 49.4 us)
Sparse Core Ops, SparseCore 0:
  3637.1 606.7 all-reduce.4
  4251.5 132.9 all-reduce.6
where the time goes:
time: 4440 us; the launch traced here: 4400 us
  waiting for transfers between devices  3060 us (69%)
  blocking collectives  593 us (13%)
  starting transfers between devices  284 us (6%)
  loops' own time  160 us (4%)
  matrix products  111 us (2%)
  other arithmetic  104 us (2%)
  local copies, waits for them, and re-layouts  69.6 us (2%)
    ppermute x12, waiting for transfers between devices, from_behind(): return lax.ppermute(block, axis, route)  2920 us
    psum x1, blocking collectives, combine(): lax.psum((block_terms[0], block_terms[1], block_terms[2]), ('pipe', 'dp'))  573 us
    ppermute x12, starting transfers between devices, from_behind(): return lax.ppermute(block, axis, route)  283 us
    psum x1, waiting for transfers between devices, combine(): lax.psum((block_terms[0], block_terms[1], block_terms[2]), ('pipe', 'dp'))  141 us
  transfers between devices with their start and end apart: 14, of which 13 were waited for; matrix products, arithmetic and copies ran while one was open for 1% of the time, Pallas kernels for 0%

commit v1 on v0

v1 whole, which is shorter than its diff:
```python
import functools
import math

import jax
import jax.numpy as jnp
import ml_dtypes
import numpy as np
from jax import lax
from jax.experimental import pallas as pl
from jax.experimental.pallas import tpu as pltpu
from jax.sharding import PartitionSpec as P

HEADS = 8
HEAD = 32
KS = 7
R_SIDE = 14
C_SIDE = 20
PIX = 280
SPAN = 13
EPS = 1e-05
NEG = -1e30
HALF = 144
PAD = 288
OWN = 140
LAG = 1
LATE_PAIR = 3
QUERY_AT = (0, 136)
KEY_AT = (0, 32)
LOG2E = math.log2(math.e)
LN2 = math.log(2.0)
F32 = jnp.float32
BF16 = jnp.bfloat16


def token_places(dilation):
    place = np.arange(PIX)
    if dilation == 1:
        return place // C_SIDE, place % C_SIDE
    row_class, rest = place // OWN, place % OWN
    row_local, rest = rest // C_SIDE, rest % C_SIDE
    col_class, col_local = rest // 10, rest % 10
    return row_local * 2 + row_class, col_local * 2 + col_class


def line_window(q, k, dilation, length):
    same = (q % dilation) == (k % dilation)
    count = (length - q % dilation + dilation - 1) // dilation
    start = np.clip(q // dilation - KS // 2, 0, count - KS)
    reach = k // dilation - start
    return same & (reach >= 0) & (reach < KS)


def constant_tables():
    window = np.zeros((2, 2, HALF, 256), np.float32)
    lane_row = np.full((2, 2, 8, 256), 1000, np.int32)
    lane_col = np.full((2, 2, 8, 256), 1000, np.int32)
    perm = np.zeros((2, PAD, PAD), np.float32)
    for d in (1, 2):
        rows, cols = token_places(d)
        perm[d - 1, np.arange(PIX), rows * C_SIDE + cols] = 1
        for half in (0, 1):
            keys = KEY_AT[half] + np.arange(256)
            real = keys < PIX
            key_row = np.where(real, rows[np.minimum(keys, PIX - 1)], 1000)
            key_col = np.where(real, cols[np.minimum(keys, PIX - 1)], 1000)
            query = half * OWN + np.arange(OWN)
            inside = (
                line_window(rows[query][:, None], key_row[None], d, R_SIDE)
                & line_window(cols[query][:, None], key_col[None], d, C_SIDE)
                & real[None]
            )
            window[d - 1, half, query - QUERY_AT[half]] = np.where(inside, 0.0, NEG)
            lane_row[d - 1, half] = key_row[None]
            lane_col[d - 1, half] = key_col[None]
    pick = np.zeros((2, 256, 512), np.float32)
    for m in range(-6, 7):
        for w in range(-6, 7):
            gap = 20 * m + w
            for turn in (0, 1):
                entry = (m + 6) * SPAN + w + 6 if turn == 0 else (w + 6) * SPAN + m + 6
                for half in (0, 1):
                    pick[turn, entry, half * 256 + (gap + QUERY_AT[half] - KEY_AT[half]) % 256] = 1
    low = ml_dtypes.bfloat16
    return (
        window.astype(low),
        lane_row,
        lane_col,
        perm.astype(low),
        perm.transpose(0, 2, 1).astype(low),
        pick.astype(low),
    )


def dot_nn(a, b):
    return lax.dot_general(a, b, (((1,), (0,)), ((), ())), preferred_element_type=F32)


def dot_nt(a, b):
    return lax.dot_general(a, b, (((1,), (1,)), ((), ())), preferred_element_type=F32)


def dot_tn(a, b):
    return lax.dot_general(a, b, (((0,), (0,)), ((), ())), preferred_element_type=F32)


def lane_ids(shape):
    return lax.broadcasted_iota(jnp.int32, shape, len(shape) - 1)


def normalise(x):
    center = x - jnp.mean(x, axis=-1, keepdims=True)
    rstd = lax.rsqrt(jnp.mean(center * center, axis=-1, keepdims=True) + EPS)
    return center * rstd, rstd


def gelu_pair(h):
    phi = 0.5 + 0.5 * lax.erf(h * math.sqrt(0.5))
    e = jnp.exp2(h * h * (-0.5 * LOG2E))
    return h * phi, phi + h * (e * (1.0 / math.sqrt(2.0 * math.pi)))


def mask_heads(rows):
    lanes = lane_ids((1, 256)) // HEAD
    return jnp.concatenate([rows * jnp.where(lanes == h, 1.0, 0.0).astype(BF16) for h in range(HEADS)], axis=0)


def pick_heads(stack):
    lanes = lane_ids((HALF, 128)) // HEAD
    total = stack[0:HALF]
    for h in range(1, 4):
        total = jnp.where(lanes == h, stack[h * HALF : (h + 1) * HALF], total)
    return total


def diagonal_sums(left, right):
    lanes = lane_ids((8, 128))
    low = jnp.zeros((8, 128), F32)
    high = jnp.zeros((8, 128), F32)
    for t in range(HALF // 8):
        shift = (8 * t) % 128
        a = left[8 * t : 8 * t + 8]
        b = right[8 * t : 8 * t + 8]
        if 8 * t >= 128:
            a, b = b, a
        if shift:
            a = pltpu.roll(a, 128 - shift, 1)
            b = pltpu.roll(b, 128 - shift, 1)
            near = lanes < 128 - shift
            a, b = jnp.where(near, a, b), jnp.where(near, b, a)
        low = low + a
        high = high + b
    return low, high


def together(*works):
    works = list(works)
    while works:
        for work in list(works):
            if next(work, None) is None:
                works.remove(work)


def join_halves(first, second):
    upper = lax.broadcasted_iota(jnp.int32, (8, first.shape[1]), 0) < 4
    seam = jnp.where(upper, first[136:144], second[0:8])
    tail = jnp.zeros((8, first.shape[1]), first.dtype)
    return jnp.concatenate([first[0:136], seam, second[8:144], tail], axis=0)


def own_rows(rows, half):
    upper = lax.broadcasted_iota(jnp.int32, (8, rows.shape[1]), 0) < 4
    if half == 0:
        return jnp.concatenate([rows[0:136], jnp.where(upper, rows[136:144], 0.0)], axis=0)
    return jnp.concatenate([jnp.where(upper, 0.0, rows[0:8]), rows[8:144]], axis=0)


def mesh_copy(src, dst, send, recv, pipe, dp):
    return pltpu.make_async_remote_copy(
        src_ref=src,
        dst_ref=dst,
        send_sem=send,
        recv_sem=recv,
        device_id=(pipe, dp),
        device_id_type=pl.DeviceIdType.MESH,
    )


def await_bytes(like, sem):
    pltpu.make_async_copy(like, like, sem).wait()


class Pack:
    def __init__(self, dp, refs, sems):
        self.pairs = dp // 2
        self.acc, self.send, self.core, self.side, self.cut, self.gather, self.total = refs
        self.core_send, self.core_recv, self.side_send, self.side_recv, self.cut_send, self.cut_recv = sems[0:6]
        self.all_send = sems[6:8]
        self.p = lax.axis_index("pipe")
        self.me = lax.axis_index("dp")
        self.c = lax.rem(self.p, 2)
        self.x = lax.rem(self.me, 2)
        self.z = lax.div(self.me, 2)
        self.sibling = self.p + 1 - 2 * self.c
        self.across = lax.rem(self.p + 2, 4)
        self.partner = self.me + 1 - 2 * self.x

    def owner(self, work):
        if self.pairs == 4:
            work()
        else:
            pl.when(self.z < 4)(work)

    def half(self, core):
        return pl.ds(pl.multiple_of(128 * core, 128), 128)

    def quarter(self, side):
        return pl.ds(pl.multiple_of(128 * self.c + 64 * side, 64), 64)

    def core_copy(self, k):
        return mesh_copy(
            self.send.at[k, self.half(1 - self.c)],
            self.core.at[k],
            self.core_send.at[k],
            self.core_recv.at[k],
            self.sibling,
            self.me,
        )

    def side_copy(self, k):
        return mesh_copy(
            self.send.at[k, self.quarter(1 - self.x)],
            self.side.at[k],
            self.side_send.at[k],
            self.side_recv.at[k],
            self.p,
            self.partner,
        )

    def start_core(self, k):
        self.send[k] = self.acc[k].astype(BF16)
        self.core_copy(k).start()

    def start_side(self, k):
        self.core_copy(k).wait_recv()
        rows = self.half(self.c)
        self.send[k, rows] = (self.send[k, rows].astype(F32) + self.core[k].astype(F32)).astype(BF16)
        self.side_copy(k).start()

    def start_cut(self, k):
        self.side_copy(k).wait_recv()
        summed = self.send[k, self.quarter(self.x)].astype(F32) + self.side[k].astype(F32)
        self.cut[k] = summed.astype(BF16).reshape(self.cut.shape[1:])

        @self.owner
        def _():
            self.gather[k, self.z] = self.cut[k, self.z]

        def send_piece(j, carry):
            @pl.when(j != self.z)
            def _():
                mesh_copy(
                    self.cut.at[k, j],
                    self.gather.at[k, self.z],
                    self.cut_send.at[k],
                    self.cut_recv.at[k],
                    self.p,
                    2 * j + self.x,
                ).start()

            return carry

        lax.fori_loop(0, 4, send_piece, 0)

    def sum_pieces(self, k):
        @self.owner
        def _():
            await_bytes(self.gather.at[k, pl.ds(0, self.pairs - 1)], self.cut_recv.at[k])

            def add(j, total):
                return total + self.gather[k, j].astype(F32)

            zero = jnp.zeros(self.total.shape[1:], F32)
            self.total[k] = lax.fori_loop(0, self.pairs, add, zero).astype(BF16)

    def start_gather(self, k, place, recv, pipe, far=None):
        def send_piece(j, carry):
            local = (pipe == self.p) & (j == self.z)

            @pl.when(local)
            def _():
                pltpu.make_async_copy(self.total.at[k], place, recv).start()

            @pl.when(jnp.logical_not(local))
            def _():
                mesh_copy(self.total.at[k], place, self.all_send[0].at[k], recv, pipe, 2 * j + self.x).start()

            if far is not None:

                @pl.when(far)
                def _():
                    mesh_copy(
                        self.total.at[k], place, self.all_send[1].at[k], recv, self.across, 2 * j + self.x
                    ).start()

            return carry

        @self.owner
        def _():
            lax.fori_loop(0, self.pairs, send_piece, 0)

    def finish_sends(self, k, pipe, far=None):
        self.core_copy(k).wait_send()
        self.side_copy(k).wait_send()

        @self.owner
        def _():
            await_bytes(self.cut.at[k, pl.ds(0, 3)], self.cut_send.at[k])

            @pl.when(pipe == self.p)
            def _():
                await_bytes(self.gather.at[k, pl.ds(0, self.pairs - 1)], self.all_send[0].at[k])

            @pl.when(pipe != self.p)
            def _():
                await_bytes(self.gather.at[k], self.all_send[0].at[k])

            if far is not None:

                @pl.when(far)
                def _():
                    await_bytes(self.gather.at[k], self.all_send[1].at[k])

        if self.pairs > 4:

            @pl.when(self.z >= 4)
            def _():
                await_bytes(self.cut.at[k], self.cut_send.at[k])


class Direct:
    def __init__(self, dp, refs, sems):
        self.dp = dp
        self.acc, self.send, self.core, self.cut, self.gather, self.total = refs
        self.core_send, self.core_recv, self.cut_send, self.cut_recv, self.all_send = sems
        self.p = lax.axis_index("pipe")
        self.me = lax.axis_index("dp")
        self.c = lax.rem(self.p, 2)
        self.sibling = self.p + 1 - 2 * self.c
        self.goal = self.p - self.c

    def owner(self, work):
        if self.dp == 8:
            work()
        else:
            pl.when(self.me < 8)(work)

    def half(self, core):
        return pl.ds(pl.multiple_of(128 * core, 128), 128)

    def core_copy(self):
        source = self.send.at[self.half(1 - self.c)]
        return mesh_copy(source, self.core, self.core_send, self.core_recv, self.sibling, self.me)

    def start_core(self):
        self.send[...] = self.acc[...].astype(BF16)
        self.core_copy().start()

    def start_cut(self):
        self.core_copy().wait_recv()
        summed = self.send[self.half(self.c)].astype(F32) + self.core[...].astype(F32)
        self.cut[...] = summed.astype(BF16).reshape(self.cut.shape)

        @self.owner
        def _():
            self.gather[self.me] = self.cut[self.me]

        def send_piece(j, carry):
            @pl.when(j != self.me)
            def _():
                place = self.gather.at[self.me]
                mesh_copy(self.cut.at[j], place, self.cut_send, self.cut_recv, self.p, j).start()

            return carry

        lax.fori_loop(0, 8, send_piece, 0)

    def start_gather(self, land, recv):
        place = land.at[pl.ds(pl.multiple_of(128 * self.c + 16 * self.me, 16), 16)]

        def send_piece(j, carry):
            local = (self.c == 0) & (j == self.me)

            @pl.when(local)
            def _():
                pltpu.make_async_copy(self.total, place, recv).start()

            @pl.when(jnp.logical_not(local))
            def _():
                mesh_copy(self.total, place, self.all_send, recv, self.goal, j).start()

            return carry

        @self.owner
        def _():
            await_bytes(self.gather.at[pl.ds(0, self.dp - 1)], self.cut_recv)

            def add(j, total):
                return total + self.gather[j].astype(F32)

            self.total[...] = lax.fori_loop(0, self.dp, add, jnp.zeros(self.total.shape, F32)).astype(BF16)
            lax.fori_loop(0, self.dp, send_piece, 0)

    def finish_sends(self):
        self.core_copy().wait_send()

        @self.owner
        def _():
            await_bytes(self.cut.at[pl.ds(0, 7)], self.cut_send)

            @pl.when(self.c == 0)
            def _():
                await_bytes(self.gather.at[pl.ds(0, self.dp - 1)], self.all_send)

            @pl.when(self.c == 1)
            def _():
                await_bytes(self.gather, self.all_send)

        if self.dp > 8:

            @pl.when(self.me >= 8)
            def _():
                await_bytes(self.cut, self.cut_send)


def section_kernel(
    images,
    dp,
    mask_ref,
    turn_ref,
    dil_ref,
    tok_hbm,
    cot_hbm,
    win_hbm,
    gain_ref,
    shift_ref,
    bin_ref,
    bout_ref,
    table_ref,
    proj_hbm,
    down_hbm,
    window_hbm,
    lrow_hbm,
    lcol_hbm,
    perm_hbm,
    permt_hbm,
    pick_hbm,
    out_hbm,
    back_hbm,
    sum_in_hbm,
    sum_down_hbm,
    notes_hbm,
    land_in,
    land_down,
    notes_ref,
    proj_ref,
    down_ref,
    window_ref,
    lrow_ref,
    lcol_ref,
    perm_ref,
    permt_ref,
    pick_ref,
    nat_ref,
    xhat_ref,
    rstd_ref,
    qkv_ref,
    prob_ref,
    att_ref,
    act_ref,
    slope_ref,
    up_ref,
    inverse_ref,
    ones_ref,
    maskadd_ref,
    bias_ref,
    tab_ref,
    diag_ref,
    win_ref,
    small_ref,
    gs_ref,
    give_ref,
    load_ref,
    wide_acc,
    wide_send,
    wide_core,
    wide_side,
    wide_cut,
    wide_gather,
    wide_total,
    slim_acc,
    slim_send,
    slim_core,
    slim_side,
    slim_cut,
    slim_gather,
    slim_total,
    tall_send,
    tall_core,
    tall_cut,
    tall_gather,
    tall_total,
    note_send,
    note_core,
    note_side,
    note_all,
    note_far,
    load_sem,
    const_sems,
    win_sems,
    small_sems,
    give_send,
    give_recv,
    cross_send,
    cross_recv,
    wide_sems,
    slim_sems,
    tall_sems,
    land_sems,
    share_send,
    share_recv,
    side_send,
    side_recv,
    far_send,
    far_recv,
    note_sems,
):
    p = lax.axis_index("pipe")
    me = lax.axis_index("dp")
    core = lax.rem(p, 2)
    block = lax.div(p, 2)
    sibling = p + 1 - 2 * core
    across = lax.rem(p + 2, 4)
    first = core * images
    rows_own = images * PIX
    pair_rows = 2 * PIX
    wide = Pack(
        dp,
        (wide_acc.at[pl.ds(1, 1)], wide_send, wide_core, wide_side, wide_cut, wide_gather, wide_total),
        [wide_sems.at[n] for n in range(8)],
    )
    slim = Pack(
        dp,
        (slim_acc, slim_send, slim_core, slim_side, slim_cut, slim_gather, slim_total),
        [slim_sems.at[n] for n in range(8)],
    )
    tall = Direct(
        dp,
        (wide_acc.at[0], tall_send, tall_core, tall_cut, tall_gather, tall_total),
        [tall_sems.at[n] for n in range(5)],
    )

    constants = (
        (window_hbm, window_ref),
        (lrow_hbm, lrow_ref),
        (lcol_hbm, lcol_ref),
        (perm_hbm, perm_ref),
        (permt_hbm, permt_ref),
        (proj_hbm.at[block], proj_ref),
        (down_hbm.at[block], down_ref),
    )
    constants = [
        pltpu.make_async_copy(source, target, const_sems.at[n]) for n, (source, target) in enumerate(constants)
    ]
    pick_load = pltpu.make_async_copy(pick_hbm, pick_ref, const_sems.at[len(constants)])

    barrier = pltpu.get_barrier_semaphore()
    side = lax.rem(me, 2)
    pair_of = lax.div(me, 2)
    partner = me + 1 - 2 * side

    def greet_one(pipe, dp_index):
        pl.semaphore_signal(
            barrier, inc=1, device_id=(pipe, dp_index), device_id_type=pl.DeviceIdType.MESH
        )

    def greet(j, carry):
        greet_one(sibling, j)
        pl.when(j != me)(lambda: greet_one(p, j))
        pl.when(lax.rem(j, 2) == side)(lambda: greet_one(across, j))
        return carry

    lax.fori_loop(0, dp, greet, 0)

    mine = pl.ds(pl.multiple_of(core * rows_own, 16), rows_own)
    win_load = pltpu.make_async_copy(win_hbm.at[0], win_ref.at[core], load_sem.at[0])
    win_load.start()
    pick_load.start()
    tok_load = pltpu.make_async_copy(tok_hbm.at[mine], load_ref, load_sem.at[1])
    cot_load = pltpu.make_async_copy(cot_hbm.at[mine], load_ref, load_sem.at[1])
    pl.when(block == 0)(tok_load.start)
    pl.when(block == 1)(cot_load.start)
    for copy in constants:
        copy.start()
    small_ref[core, 0:1] = gain_ref[...].astype(F32)
    small_ref[core, 1:2] = shift_ref[...].astype(F32)
    small_ref[core, 2:3] = bout_ref[...].astype(F32)
    for part in range(3):
        small_ref[core, 3 + part : 4 + part] = bin_ref[:, part * 256 : part * 256 + 256].astype(F32)
    pl.semaphore_wait(barrier, 2 * dp - 1 + dp // 2)
    win_copy = mesh_copy(win_ref.at[core], win_ref.at[core], win_sems.at[0], win_sems.at[1], sibling, me)
    small_copy = mesh_copy(
        small_ref.at[core], small_ref.at[core], small_sems.at[0], small_sems.at[1], sibling, me
    )
    small_copy.start()
    win_load.wait()
    win_copy.start()

    tab_ref[...] = jnp.zeros_like(tab_ref)
    tab_ref[:, 0 : SPAN * SPAN] = table_ref[block].astype(F32)
    tab = tab_ref[...].astype(BF16)
    pick_load.wait()
    for turn in range(2):
        base = dot_nn(tab, pick_ref[turn]) * LOG2E
        for s in range(8):
            rows = pl.ds(turn * 8, 8)
            for half in range(2):
                ring = base[:, half * 256 : half * 256 + 256]
                ring = pltpu.roll(ring, s, 1) if s else ring
                diag_ref[2 * half, rows, s] = ring[:, 0:128]
                diag_ref[2 * half + 1, rows, s] = ring[:, 128:256]

    def spread(n, carry):
        lanes = lane_ids((8, 128))
        for half in range(2):
            for t in range(HALF // 8):
                shift = (8 * t) % 128
                x, z = diag_ref[2 * half, n], diag_ref[2 * half + 1, n]
                if 8 * t >= 128:
                    x, z = z, x
                if shift:
                    x, z = pltpu.roll(x, shift, 1), pltpu.roll(z, shift, 1)
                    x, z = jnp.where(lanes >= shift, x, z), jnp.where(lanes >= shift, z, x)
                rows = pl.ds(8 * t, 8)
                bias_ref[n, half, 0, rows] = x
                bias_ref[n, half, 1, rows] = z
        return carry

    lax.fori_loop(0, 16, spread, 0)
    tok_load.wait()

    def load_pair(pair):
        rows = load_ref[pl.ds(pair * pair_rows, pair_rows)].astype(F32)
        for n in range(2):
            one = rows[n * PIX : n * PIX + PIX]
            nat_ref[0, 2 * pair + n] = jnp.concatenate([one, jnp.zeros((8, 256), F32)], axis=0).astype(BF16)

    def late_start():
        head_of_row = lax.broadcasted_iota(jnp.int32, (256, 1024), 0) // HEAD
        head_of_lane = lane_ids((256, 1024)) // 128
        ones_ref[...] = jnp.where(head_of_row == head_of_lane, 1.0, 0.0).astype(BF16)
        diag_ref[...] = jnp.zeros_like(diag_ref)
        gs_ref[...] = jnp.zeros_like(gs_ref)
        wide_acc[...] = jnp.zeros_like(wide_acc)
        slim_acc[...] = jnp.zeros_like(slim_acc)
        for pair in range(1, images // 2):
            load_pair(pair)

    load_pair(0)
    pl.when(block == 1)(late_start)
    for copy in constants:
        copy.wait()
    await_bytes(small_ref.at[0], small_sems.at[1])
    await_bytes(win_ref.at[0], win_sems.at[1])

    def spacing(i):
        return jnp.maximum(dil_ref[block, first + i] - 1, 0)

    def mask_for(i):
        d = spacing(i)
        rows_valid = mask_ref[first + i, 0]
        for r in range(1, R_SIDE):
            rows_valid = rows_valid + mask_ref[first + i, r * C_SIDE]
        cols_valid = mask_ref[first + i, 0]
        for c in range(1, C_SIDE):
            cols_valid = cols_valid + mask_ref[first + i, c]
        for half in range(2):
            allowed = (lrow_ref[d, half] < rows_valid) & (lcol_ref[d, half] < cols_valid)
            shut = jnp.where(allowed, 0.0, NEG)[0:1]
            maskadd_ref[half] = window_ref[d, half].astype(F32) + shut

    def give_copies(kind, pair):
        target = pl.ds(pl.multiple_of(core * rows_own + pair * pair_rows, 16), pair_rows)
        target = (out_hbm, back_hbm)[kind // 2].at[0, target]
        source = give_ref.at[kind, pair, pl.ds(0, pair_rows)]
        recv = give_recv.at[kind // 2]
        remote = mesh_copy(source, target, give_send.at[kind, pair], recv, sibling, me)
        local = pltpu.make_async_copy(source, target, recv)
        return remote, local

    def cross_copy(i):
        return mesh_copy(nat_ref.at[0, i], nat_ref.at[1, i], cross_send.at[i], cross_recv.at[i], across, me)

    def record(kind, i, low):
        give_ref[kind, lax.div(i, 2), pl.ds(pl.multiple_of(lax.rem(i, 2) * PAD, 16), PAD)] = low

    def cross(kind, i):
        low = give_ref[kind, lax.div(i, 2), pl.ds(pl.multiple_of(lax.rem(i, 2) * PAD, 16), PAD)]
        nat_ref[0, i] = dot_nn(permt_ref[spacing(i)], low).astype(BF16)
        cross_copy(i).start()

    def await_cross(i):
        await_bytes(nat_ref.at[1, i], cross_recv.at[i])

    def deliver(kind, pair):
        rows = []
        for n in range(2):
            low = give_ref[kind, pair, n * PAD : n * PAD + PAD]
            rows.append(dot_nn(permt_ref[spacing(2 * pair + n)], low)[0:PIX])
        give_ref[kind, pair, 0:pair_rows] = jnp.concatenate(rows, axis=0).astype(BF16)
        remote, local = give_copies(kind, pair)
        pl.when(core != kind % 2)(remote.start)
        pl.when(core == kind % 2)(local.start)

    def deliver_all(kind, start):
        def one(pair, carry):
            deliver(kind, pair)
            return carry

        lax.fori_loop(start, images // 2, one, 0)

    def forward(i):
        d = spacing(i)
        turn = turn_ref[first + i]
        mask_for(i)
        x = dot_nn(perm_ref[d], nat_ref[block, i])
        xhat, rstd = normalise(x)
        xhat_ref[0, i] = xhat
        rstd_ref[0, i] = rstd
        normed = (xhat * small_ref[0, 0:1] + small_ref[0, 1:2]).astype(BF16)
        mixed = dot_nn(normed, win_ref[0])
        scaled = (mixed[:, 0:256] + small_ref[0, 3:4]) * (HEAD**-0.5 * LOG2E)
        qkv_ref[i, :, 0:256] = scaled.astype(BF16)
        qkv_ref[i, :, 256:512] = (mixed[:, 256:512] + small_ref[0, 4:5]).astype(BF16)
        qkv_ref[i, :, 512:768] = (mixed[:, 512:768] + small_ref[0, 5:6]).astype(BF16)
        ones = jnp.ones((256, 128), BF16)
        attended = []
        inverse = []
        for half in range(2):
            yield True
            query = scaled[QUERY_AT[half] : QUERY_AT[half] + HALF].astype(BF16)
            key_rows = pl.ds(KEY_AT[half], 256)
            scores = dot_nt(mask_heads(query), qkv_ref[i, key_rows, 256:512])
            for h in range(HEADS):
                n = turn * 8 + h
                part = scores[h * HALF : (h + 1) * HALF]
                left = part[:, 0:128] + (bias_ref[n, half, 0] + maskadd_ref[half, :, 0:128])
                right = part[:, 128:256] + (bias_ref[n, half, 1] + maskadd_ref[half, :, 128:256])
                top = jnp.max(jnp.maximum(left, right), axis=-1, keepdims=True)
                rows = pl.ds(h * HALF, HALF)
                prob_ref[i, half, rows, 0:128] = jnp.exp2(left - top).astype(BF16)
                prob_ref[i, half, rows, 128:256] = jnp.exp2(right - top).astype(BF16)
            yield True
            values = []
            inverses = []
            for part in range(2):
                right = jnp.concatenate([qkv_ref[i, key_rows, 512 + part * 128 : 640 + part * 128], ones], axis=1)
                stack = dot_nn(prob_ref[i, half, pl.ds(part * 4 * HALF, 4 * HALF)], right)
                inverses.append(1.0 / pick_heads(stack[:, 128:256]))
                values.append(pick_heads(stack[:, 0:128]) * inverses[part])
            attended.append(jnp.concatenate(values, axis=1))
            inverse.append(jnp.where(lane_ids((HALF, 128)) % HEAD < 16, inverses[0], inverses[1]))
        att_ref[i] = join_halves(*attended).astype(BF16)
        inverse_ref[i] = join_halves(*inverse)
        y = (x + dot_nn(att_ref[i], proj_ref[...]) + small_ref[0, 2:3]).astype(BF16)
        record(0, i, y)
        yield True
        x = y.astype(F32)
        xhat, rstd = normalise(x)
        xhat_ref[1, i] = xhat
        rstd_ref[1, i] = rstd
        normed = (xhat * small_ref[1, 0:1] + small_ref[1, 1:2]).astype(BF16)
        for part in range(3):
            yield True
            cols = slice(part * 256, part * 256 + 256)
            hidden = dot_nn(normed, win_ref[1, :, cols]) + small_ref[1, 3 + part : 4 + part]
            active, slope = gelu_pair(hidden)
            act_ref[i, :, cols] = active.astype(BF16)
            slope_ref[i, :, cols] = slope.astype(BF16)
        yield True
        z = (x + dot_nn(act_ref[i], down_ref[...]) + small_ref[1, 2:3]).astype(BF16)
        record(1, i, z)

    def norm_backward(i, t, g, dmix):
        dn = dot_nt(dmix, win_ref[t])
        xhat = xhat_ref[t, i]
        gs_ref[t, 0:1] += jnp.sum(dn * xhat, axis=0, keepdims=True)
        gs_ref[t, 1:2] += jnp.sum(dn, axis=0, keepdims=True)
        gs_ref[t, 2:3] += jnp.sum(g, axis=0, keepdims=True)
        e = dn * small_ref[t, 0:1]
        first_mean = jnp.mean(e, axis=-1, keepdims=True)
        second_mean = jnp.mean(e * xhat, axis=-1, keepdims=True)
        return (g + (e - first_mean - xhat * second_mean) * rstd_ref[t, i]).astype(BF16)

    def feed_backward(i):
        g = dot_nn(perm_ref[spacing(i)], nat_ref[1 - block, i])
        low = g.astype(BF16)
        nat_ref[1, i] = low
        for part in range(3):
            yield True
            cols = slice(part * 256, part * 256 + 256)
            dact = dot_nt(low, down_ref[cols])
            dhidden = dact * slope_ref[i, :, cols].astype(F32)
            gs_ref[1, 3 + part : 4 + part] += jnp.sum(dhidden, axis=0, keepdims=True)
            slope_ref[i, :, cols] = dhidden.astype(BF16)
        yield True
        result = norm_backward(i, 1, g, slope_ref[i])
        up_ref[i] = result
        record(3, i, result)

    def attention_backward(i):
        turn = turn_ref[first + i].astype(F32)
        low = up_ref[i]
        packed = inverse_ref[i]
        lanes = lane_ids(packed.shape) % HEAD
        inverse = jnp.concatenate(
            [
                jnp.where(lanes < 16, packed, pltpu.roll(packed, 16, 1)),
                jnp.where(lanes < 16, pltpu.roll(packed, 112, 1), packed),
            ],
            axis=1,
        )
        datt_all = dot_nt(low, proj_ref[...]) * inverse
        attended = att_ref[i].astype(F32)
        query_all = qkv_ref[i, :, 0:256].astype(F32)
        dqueries = []
        dkvs = []
        for half in range(2):
            yield True
            rows_half = slice(QUERY_AT[half], QUERY_AT[half] + HALF)
            key_rows = pl.ds(KEY_AT[half], 256)
            datt32 = own_rows(datt_all[rows_half], half)
            datt = datt32.astype(BF16)
            query_t = query_all[rows_half].astype(BF16).T
            datt_t = datt.T
            dprob = dot_nt(mask_heads(datt), qkv_ref[i, key_rows, 512:768])
            totals = dot_nn((datt32 * attended[rows_half]).astype(BF16), ones_ref[...])
            dkeys = []
            dvalues = []
            ds = []
            for h in range(HEADS):
                rows = pl.ds(h * HALF, HALF)
                prob = prob_ref[i, half, rows]
                total = totals[:, h * 128 : h * 128 + 128]
                part = dprob[h * HALF : (h + 1) * HALF]
                left = prob[:, 0:128].astype(F32) * (part[:, 0:128] - total)
                right = prob[:, 128:256].astype(F32) * (part[:, 128:256] - total)
                for kind, value in enumerate(diagonal_sums(left, right)):
                    diag_ref[2 * half + kind, h] += value * (1.0 - turn)
                    diag_ref[2 * half + kind, 8 + h] += value * turn
                ds.append(jnp.concatenate([left.astype(BF16), right.astype(BF16)], axis=1))
                head_rows = slice(h * HEAD, (h + 1) * HEAD)
                dkeys.append(dot_nn(query_t[head_rows], ds[h]))
                dvalues.append(dot_nn(datt_t[head_rows], prob))
            parts = []
            for part in range(2):
                keys = qkv_ref[i, key_rows, 256 + part * 128 : 384 + part * 128]
                parts.append(pick_heads(dot_nn(jnp.concatenate(ds[4 * part : 4 * part + 4], axis=0), keys)))
            dqueries.append(jnp.concatenate(parts, axis=1))
            yield True
            dkeys = jnp.concatenate(dkeys, axis=0).T * LN2
            dvalues = jnp.concatenate(dvalues, axis=0).T
            dkvs.append(jnp.concatenate([dkeys, dvalues], axis=1))
        yield True
        dquery = join_halves(*dqueries) * HEAD**-0.5
        dkv = jnp.concatenate([dkvs[0][0:32], dkvs[0][32:256] + dkvs[1][0:224], dkvs[1][224:256]], axis=0)
        gs_ref[0, 3:4] += jnp.sum(dquery, axis=0, keepdims=True)
        gs_ref[0, 4:5] += jnp.sum(dkv[:, 0:256], axis=0, keepdims=True)
        gs_ref[0, 5:6] += jnp.sum(dkv[:, 256:512], axis=0, keepdims=True)
        qkv_ref[i, :, 0:256] = dquery.astype(BF16)
        qkv_ref[i, :, 256:768] = dkv.astype(BF16)
        yield True
        result = norm_backward(i, 0, low.astype(F32), qkv_ref[i])
        record(2, i, result)

    def early_sides():
        slim.start_side(0)
        wide.start_side(0)

    def add_in(t, at, count):
        rows = count * PAD
        dmix = (qkv_ref, slope_ref)[t][pl.ds(at, count)].reshape(rows, 768)
        xhat = xhat_ref[t, pl.ds(at, count)].reshape(rows, 256)
        normed = (xhat * small_ref[t, 0:1] + small_ref[t, 1:2]).astype(BF16)
        wide_acc[t] += dot_tn(normed, dmix)

    def add_feed(at, count):
        rows = count * PAD
        up = nat_ref[1, pl.ds(at, count)].reshape(rows, 256)
        for part in range(3):
            cols = slice(part * 256, part * 256 + 256)
            slim_acc[0, :, cols] += dot_tn(act_ref[pl.ds(at, count), :, cols].reshape(rows, 256), up)
        add_in(1, at, count)
        after = up_ref[pl.ds(at, count)].reshape(rows, 256)
        slim_acc[0, :, 768:1024] += dot_tn(att_ref[pl.ds(at, count)].reshape(rows, 256), after)

    def start_feed():
        slim.start_core(0)
        wide.start_core(0)

    def backward(i):
        yield from feed_backward(i)
        yield from attention_backward(i)

    def feed_and_sums(i):
        yield from feed_backward(i)
        yield True
        add_feed(i, 1)

    def attention_and_sums(i):
        yield from attention_backward(i)
        yield True
        add_in(0, i, 1)

    def over(start, stop, work):
        def one(i, carry):
            work(i)
            return carry

        lax.fori_loop(start, stop, one, 0)

    def first_forward(i):
        pl.when(block == 1)(lambda: await_cross(i))
        together(forward(i))

        @pl.when(block == 0)
        def _():
            cross(1, i)
            pl.when(i == 0)(late_start)

            @pl.when(lax.rem(i, 2) == 1)
            def _():
                deliver(0, lax.div(i, 2))
                deliver(1, lax.div(i, 2))

    over(0, jnp.where(block == 0, images, 1), first_forward)

    def back_and_forth(i):
        await_cross(i + 1)
        together(backward(i), forward(i + 1))
        cross(2, i)

    over(0, jnp.where(block == 0, 0, images - 1), back_and_forth)

    def early_feed(i):
        await_cross(i)
        together(feed_and_sums(i))

        @pl.when(lax.rem(i, 2) == 1)
        def _():
            pl.when(i < images - 1)(lambda: deliver(3, lax.div(i, 2)))

    over(0, jnp.where(block == 0, LAG, 0), early_feed)

    def both_backward(i):
        await_cross(i)
        together(feed_and_sums(i), attention_and_sums(i - LAG))
        pl.when(lax.rem(i, 2) == 1)(lambda: deliver(3, lax.div(i, 2)))
        pl.when((lax.rem(i, 2) == 1) & (i >= 3))(lambda: deliver(2, lax.div(i - 3, 2)))

    over(LAG, jnp.where(block == 0, images - 1, LAG), both_backward)
    over(jnp.where(block == 0, images - 1, images), images, early_feed)

    @pl.when(block == 0)
    def _():
        start_feed()
        deliver(3, images // 2 - 1)
        deliver(2, images // 2 - 2)
        early_sides()
        together(attention_and_sums(images - 2), attention_and_sums(images - 1))
        slim.start_cut(0)

    @pl.when(block == 1)
    def _():
        together(backward(images - 1))
        cross(2, images - 1)
        over(0, images // 4, lambda n: add_feed(4 * n, 4))
        start_feed()
        over(0, images // 4, lambda n: add_in(0, 4 * n, 4))
        early_sides()
        tall.start_core()
        deliver_all(3, 0)
        slim.start_cut(0)
        deliver_all(0, 0)

    piece_rows = pl.ds(pl.multiple_of(pair_of * 16, 16), 16)
    quarter_rows = pl.ds(pl.multiple_of(128 * core + 64 * side + 16 * pair_of, 16), 16)
    far = block == 0
    pl.when(block == 0)(tall.start_core)
    wide.start_cut(0)

    table_sum = jnp.zeros((8, 256), F32)
    for turn in range(2):
        rows = pl.ds(turn * 8, 8)
        sums = []
        for half in range(2):
            total = jnp.zeros((8, 256), F32)
            for s in range(8):
                ring = jnp.concatenate([diag_ref[2 * half, rows, s], diag_ref[2 * half + 1, rows, s]], axis=1)
                total = total + (pltpu.roll(ring, 256 - s, 1) if s else ring)
            sums.append(total)
        sums = jnp.concatenate(sums, axis=1)
        upper = sums.astype(BF16)
        lower = (sums - upper.astype(F32)).astype(BF16)
        table_sum = table_sum + dot_nt(upper, pick_ref[turn]) + dot_nt(lower, pick_ref[turn])

    note_send[0:8] = gs_ref[1 - core]
    note_send[8:16] = table_sum
    note_core[core, 0:8] = gs_ref[core]
    note_core[core, 8:16] = table_sum
    note_copy = mesh_copy(note_send, note_core.at[core], note_sems.at[0], note_sems.at[1], sibling, me)
    note_copy.start()
    tall.start_cut()
    slim.sum_pieces(0)
    slim.start_gather(0, land_down.at[block, core, side, piece_rows], land_sems.at[1, block], p, far)
    wide.sum_pieces(0)
    wide.start_gather(0, land_in.at[quarter_rows], land_sems.at[0, 1], 2 * block + 1)
    note_copy.wait_recv()
    note_side[side] = note_core[0] + note_core[1]
    side_copy = mesh_copy(note_side.at[side], note_side.at[side], note_sems.at[2], note_sems.at[3], p, partner)
    side_copy.start()

    def side_share(b):
        land = land_down.at[b, core, side]
        return mesh_copy(land, land, side_send.at[0, b], side_recv.at[0, b], p, partner)

    def side_start(b):
        await_bytes(land_down.at[b, 0, 0], land_sems.at[1, b])
        side_share(b).start()

    side_start(block)
    deliver_all(2, jnp.where(block == 0, LATE_PAIR, 0))
    deliver_all(1, jnp.where(block == 0, images // 2, 0))
    side_copy.wait_recv()
    note_all[pair_of] = note_side[0] + note_side[1]

    def send_note(j, carry):
        @pl.when(j != pair_of)
        def _():
            place = note_all.at[pair_of]
            mesh_copy(place, place, note_sems.at[4], note_sems.at[5], p, 2 * j + side).start()

        return carry

    lax.fori_loop(0, dp // 2, send_note, 0)

    def share_copy(b):
        land = land_down.at[b, core]
        return mesh_copy(land, land, share_send.at[b], share_recv.at[b], sibling, me)

    tall.start_gather(land_in, land_sems.at[0, 0])
    def cross_share():
        land = land_down.at[1, core]
        return mesh_copy(land, land, far_send, far_recv, across, me)

    side_share(block).wait_recv()
    share_copy(block).start()
    pl.when(block == 1)(lambda: cross_share().start())
    await_bytes(note_all.at[pl.ds(0, dp // 2 - 1)], note_sems.at[5])

    def add_note(j, total):
        return total + note_all[j]

    notes = lax.fori_loop(0, dp // 2, add_note, jnp.zeros((16, 256), F32))
    notes_ref[0] = notes[0:8]
    note_far[0] = notes[8:16]
    far_copy = mesh_copy(note_far.at[0], note_far.at[1], note_sems.at[6], note_sems.at[7], across, me)
    far_copy.start()

    def in_copies():
        copies = []
        for c in range(2):
            rows = land_in.at[pl.ds(pl.multiple_of(128 * c + 64 * side, 64), 64)]
            copies.append(mesh_copy(rows, rows, side_send.at[2, c], side_recv.at[2, c], p, partner))
        return copies

    @pl.when(core == 1)
    def _():
        await_bytes(land_in.at[0:128], land_sems.at[0, 1])
        for copy in in_copies():
            copy.start()

    @pl.when(block == 1)
    def _():
        side_start(0)
        side_share(0).wait_recv()

    pl.when(block == 0)(lambda: cross_share().wait_recv())
    share_copy(1 - block).start()
    far_copy.wait_recv()
    notes_ref[1 + block] = note_far[0]
    notes_ref[2 - block] = note_far[1]
    notes_copy = pltpu.make_async_copy(notes_ref, notes_hbm, load_sem.at[4])
    notes_copy.start()

    pl.when(core == 0)(lambda: await_bytes(land_in, land_sems.at[0, 0]))

    @pl.when(core == 1)
    def _():
        for copy in in_copies():
            copy.wait()

    results = [notes_copy, pltpu.make_async_copy(land_in, sum_in_hbm, load_sem.at[0])]
    results[1].start()
    for b in (1, 0):
        share_copy(b).wait()
        results.append(pltpu.make_async_copy(land_down.at[b], sum_down_hbm.at[b], load_sem.at[2 + b]))
        results[-1].start()
    await_bytes(out_hbm, give_recv.at[0])
    await_bytes(back_hbm, give_recv.at[1])
    for kind in range(4):

        @pl.when(core != kind % 2)
        def _(kind=kind):
            for pair in range(images // 2):
                give_copies(kind, pair)[0].wait_send()

    for i in range(images):
        cross_copy(i).wait_send()
    win_copy.wait_send()
    small_copy.wait_send()
    note_copy.wait_send()
    side_copy.wait_send()
    far_copy.wait_send()
    await_bytes(note_all.at[pl.ds(0, dp // 2 - 1)], note_sems.at[4])
    side_share(block).wait_send()

    @pl.when(block == 1)
    def _():
        side_share(0).wait_send()
        cross_share().wait_send()

    for copy in results:
        copy.wait()
    tall.finish_sends()
    wide.finish_sends(0, 2 * block + 1)
    slim.finish_sends(0, p, far)


def result_kernel(
    out_raw,
    back_raw,
    sum_in,
    sum_down,
    notes_hbm,
    out_hbm,
    back_hbm,
    g_in_hbm,
    g_proj_hbm,
    g_down_hbm,
    g_gain_hbm,
    g_shift_hbm,
    g_bin_hbm,
    g_bout_hbm,
    g_table_hbm,
    out_buf,
    back_buf,
    in_buf,
    down_buf,
    notes,
    g_in,
    g_proj,
    g_down,
    g_gain,
    g_shift,
    g_bin,
    g_bout,
    g_table,
    load_sems,
    store_sems,
    part_sems,
):
    low = [(notes_hbm, notes), (sum_in, in_buf), (sum_down, down_buf)]
    sums = [pltpu.make_async_copy(source, target, load_sems.at[n]) for n, (source, target) in enumerate(low)]
    rows = out_buf.shape[0] // 4
    loads = []
    stores = []
    for part in range(4):
        at = pl.ds(part * rows, rows)
        for n, (raw, buf, target) in enumerate(((out_raw, out_buf, out_hbm), (back_raw, back_buf, back_hbm))):
            loads.append(pltpu.make_async_copy(raw.at[0, at], buf.at[at], part_sems.at[0, n, part]))
            stores.append(pltpu.make_async_copy(buf.at[at], target.at[0, at], part_sems.at[1, n, part]))
    for copy in sums + loads:
        copy.start()
    full = [
        (g_gain, g_gain_hbm),
        (g_shift, g_shift_hbm),
        (g_bin, g_bin_hbm),
        (g_bout, g_bout_hbm),
        (g_table, g_table_hbm),
        (g_in, g_in_hbm.at[0]),
        (g_proj, g_proj_hbm),
        (g_down, g_down_hbm),
    ]
    finals = [pltpu.make_async_copy(source, target, store_sems.at[n]) for n, (source, target) in enumerate(full)]
    sums[0].wait()
    g_gain[...] = notes[0, 0:1]
    g_shift[...] = notes[0, 1:2]
    g_bout[...] = notes[0, 2:3]
    for part in range(3):
        cols = slice(part * 256, part * 256 + 256)
        g_bin[:, cols] = notes[0, 3 + part : 4 + part]
    for b in range(2):
        g_table[b] = notes[1 + b, :, 0 : SPAN * SPAN]
    for copy in finals[0:5]:
        copy.start()
    sums[1].wait()
    g_in[...] = in_buf[...].astype(F32)
    finals[5].start()
    sums[2].wait()
    for b in range(2):
        g_proj[b] = down_buf[b, :, :, :, 768:1024].reshape(256, 256).astype(F32)
        for part in range(3):
            cols = slice(part * 256, part * 256 + 256)
            g_down[b, cols] = down_buf[b, :, :, :, cols].reshape(256, 256).astype(F32)
    finals[6].start()
    finals[7].start()
    for load, store in zip(loads, stores):
        load.wait()
        store.start()
    for store in finals + stores:
        store.wait()


def run_kernels(dp, images, smem_operands, hbm_operands, vmem_operands):
    tables = [jnp.asarray(t) for t in constant_tables()]
    rows = images * PIX
    vmem = pl.BlockSpec(memory_space=pltpu.VMEM)
    smem = pl.BlockSpec(memory_space=pltpu.SMEM)
    hbm = pl.BlockSpec(memory_space=pl.ANY)
    dma = pltpu.SemaphoreType.DMA
    raw_shape = (
        jax.ShapeDtypeStruct((1, 2 * rows, 256), BF16),
        jax.ShapeDtypeStruct((1, 2 * rows, 256), BF16),
        jax.ShapeDtypeStruct((256, 768), BF16),
        jax.ShapeDtypeStruct((2, 2, 2, 64, 1024), BF16),
        jax.ShapeDtypeStruct((3, 8, 256), F32),
    )
    out_shape = raw_shape[0:2] + (
        jax.ShapeDtypeStruct((1, 256, 768), F32),
        jax.ShapeDtypeStruct((2, 256, 256), F32),
        jax.ShapeDtypeStruct((2, 768, 256), F32),
        jax.ShapeDtypeStruct((1, 256), F32),
        jax.ShapeDtypeStruct((1, 256), F32),
        jax.ShapeDtypeStruct((1, 768), F32),
        jax.ShapeDtypeStruct((1, 256), F32),
        jax.ShapeDtypeStruct((2, HEADS, SPAN * SPAN), F32),
    )

    def pack(sums, count, columns):
        return [
            pltpu.VMEM((sums, 256, columns), F32),
            pltpu.VMEM((count, 256, columns), BF16),
            pltpu.VMEM((count, 128, columns), BF16),
            pltpu.VMEM((count, 64, columns), BF16),
            pltpu.VMEM((count, 4, 16, columns), BF16),
            pltpu.VMEM((count, dp // 2, 16, columns), BF16),
            pltpu.VMEM((count, 16, columns), BF16),
        ]

    scratch = [
        *[pltpu.VMEM(shape.shape, shape.dtype) for shape in raw_shape[2:5]],
        pltpu.VMEM((256, 256), BF16),
        pltpu.VMEM((768, 256), BF16),
        *[pltpu.VMEM(table.shape, table.dtype) for table in tables],
        pltpu.VMEM((2, images, PAD, 256), BF16),
        pltpu.VMEM((2, images, PAD, 256), F32),
        pltpu.VMEM((2, images, PAD, 1), F32),
        pltpu.VMEM((images, PAD, 768), BF16),
        pltpu.VMEM((images, 2, HEADS * HALF, 256), BF16),
        pltpu.VMEM((images, PAD, 256), BF16),
        pltpu.VMEM((images, PAD, 768), BF16),
        pltpu.VMEM((images, PAD, 768), BF16),
        pltpu.VMEM((images, PAD, 256), BF16),
        pltpu.VMEM((images, PAD, 128), F32),
        pltpu.VMEM((256, 1024), BF16),
        pltpu.VMEM((2, HALF, 256), F32),
        pltpu.VMEM((16, 2, 2, HALF, 128), F32),
        pltpu.VMEM((8, 256), F32),
        pltpu.VMEM((4, 16, 8, 128), F32),
        pltpu.VMEM((2, 256, 768), BF16),
        pltpu.VMEM((2, 8, 256), F32),
        pltpu.VMEM((2, 8, 256), F32),
        pltpu.VMEM((4, images // 2, 2 * PAD, 256), BF16),
        pltpu.VMEM((rows, 256), BF16),
        *pack(2, 1, 768),
        *pack(1, 1, 1024),
        pltpu.VMEM((256, 768), BF16),
        pltpu.VMEM((128, 768), BF16),
        pltpu.VMEM((8, 16, 768), BF16),
        pltpu.VMEM((dp, 16, 768), BF16),
        pltpu.VMEM((16, 768), BF16),
        pltpu.VMEM((16, 256), F32),
        pltpu.VMEM((2, 16, 256), F32),
        pltpu.VMEM((2, 16, 256), F32),
        pltpu.VMEM((dp // 2, 16, 256), F32),
        pltpu.VMEM((2, 8, 256), F32),
        dma((6,)),
        dma((8,)),
        dma((2,)),
        dma((2,)),
        dma((4, images // 2)),
        dma((2,)),
        dma((images,)),
        dma((images,)),
        dma((8, 1)),
        dma((8, 1)),
        dma((5,)),
        dma((3, 2)),
        dma((2,)),
        dma((2,)),
        dma((3, 2)),
        dma((3, 2)),
        dma,
        dma,
        dma((8,)),
    ]
    raw = pl.pallas_call(
        functools.partial(section_kernel, images, dp),
        out_shape=raw_shape,
        in_specs=[smem] * 3 + [hbm] * 3 + [vmem] * 5 + [hbm] * 8,
        out_specs=[hbm] * 5,
        scratch_shapes=scratch,
        compiler_params=pltpu.CompilerParams(
            vmem_limit_bytes=63 * 1024 * 1024, collective_id=0, has_side_effects=True
        ),
    )(*smem_operands, *hbm_operands, *vmem_operands, *tables)
    return pl.pallas_call(
        result_kernel,
        out_shape=out_shape,
        in_specs=[hbm] * 5,
        out_specs=[hbm] * 10,
        scratch_shapes=[
            pltpu.VMEM((2 * rows, 256), BF16),
            pltpu.VMEM((2 * rows, 256), BF16),
            *[pltpu.VMEM(shape.shape, shape.dtype) for shape in raw_shape[2:5]],
            pltpu.VMEM((256, 768), F32),
            *[pltpu.VMEM(shape.shape, F32) for shape in out_shape[3:10]],
            dma((3,)),
            dma((8,)),
            dma((2, 2, 4)),
        ],
        compiler_params=pltpu.CompilerParams(vmem_limit_bytes=63 * 1024 * 1024),
    )(*raw)


def body(
    tokens_in,
    cotangent,
    valid_mask,
    orientation,
    dilation,
    norm_gain,
    norm_bias,
    in_weight,
    in_bias,
    out_bias,
    proj_weight,
    down_weight,
    position_bias,
):
    images = valid_mask.shape[0] // 2
    results = run_kernels(
        lax.axis_size("dp"),
        images,
        (valid_mask, orientation, dilation.T),
        (tokens_in, cotangent, in_weight),
        (norm_gain, norm_bias, in_bias, out_bias, position_bias, proj_weight, down_weight),
    )
    out, back, g_in, g_proj, g_down, g_gain, g_shift, g_bin, g_bout, g_table = results
    return out, back, g_gain, g_shift, g_in, g_bin, g_bout, g_proj, g_down, g_table


def solution(mesh):
    placed = (
        P("dp", None),
        P("dp", None),
        P("dp", None),
        P("dp"),
        P("dp", None),
        P("pipe", None),
        P("pipe", None),
        P("pipe", None, None),
        P("pipe", None),
        P("pipe", None),
        P(),
        P(),
        P(),
    )
    return jax.shard_map(
        body,
        mesh=mesh,
        in_specs=placed,
        out_specs=(
            P("pipe", "dp", None),
            P("pipe", "dp", None),
            P("pipe", None),
            P("pipe", None),
            P("pipe", None, None),
            P("pipe", None),
            P("pipe", None),
            P(),
            P(),
            P(),
        ),
        check_vma=False,
    )
```

time: 4440 us -> 106 us (0.02)
  waiting for transfers between devices: 3060 us -> 0 us
  blocking collectives: 593 us -> 0 us
  starting transfers between devices: 284 us -> 0 us
  loops' own time: 160 us -> 0 us
  matrix products: 111 us -> 0 us
  Pallas kernels: 0 us -> 105 us
  other arithmetic: 104 us -> 0 us
  local copies, waits for them, and re-layouts: 69.6 us -> 0 us
    ppermute x12 -> x0, waiting for transfers between devices: 2920 us -> none  [from_behind(): return lax.ppermute(block, axis, route)]
    psum x2 -> x0, blocking collectives: 593 us -> none  [the longest x1 573 us: combine(): lax.psum((block_terms[0], block_terms[1], block_terms[2]), ('pipe', 'dp'))]
    ppermute x12 -> x0, starting transfers between devices: 283 us -> none  [from_behind(): return lax.ppermute(block, axis, route)]
    psum x2 -> x0, waiting for transfers between devices: 144 us -> none  [the longest x1 141 us: combine(): lax.psum((block_terms[0], block_terms[1], block_terms[2]), ('pipe', 'dp'))]
    dot_general x24 -> x0, matrix products: 111 us -> none  [the longest x4 40.9 us: mlp_forward(): jnp.dot(active, w_down, preferred_element_type=jnp.float32)]
    pallas_call x0 -> x2, Pallas kernels: none -> 105 us  [the longest x1 99.7 us: run_kernels(): pl.pallas_call(functools.partial(section_kernel, images, dp), out_shape=r...]
    another operation x14 -> x0, loops' own time: 97.2 us -> none  [the longest x7 50.3 us: body(): lax.cond(live, lambda: backward_at(kept[safe], upstream, safe), lambda: b...]
    unnamed x8 -> x0, loops' own time: 62.6 us -> none
  transfers between devices with their start and end apart: 14 -> 0, of which waited for: 13 -> 0; matrix products, arithmetic and copies ran while one was open for 1% -> 0% of each run, Pallas kernels for 0% -> 0%
where the time goes in v1:
time: 106 us
  Pallas kernels  105 us (99%)
    pallas_call x1, Pallas kernels, run_kernels(): pl.pallas_call(functools.partial(section_kernel, images, dp), out_shape=r...  99.7 us
    pallas_call x1, Pallas kernels, run_kernels(): pl.pallas_call(result_kernel, out_shape=out_shape, in_specs=[hbm] * 5, ou...  5.61 us

profile of v1, /device:TPU:1, one launch (start us, length us, event | category | flops | bytes accessed | tf_op | source)
XLA Modules:
  0.0 106.1 jit_solution(15102997993984034118)
XLA Ops:
  0.6 99.7 %shard_map.258 = (bf16[1,4480,256]{2,1,0:T(8,128)(2,1)}, bf16[1,4480,256]{2,1,0:T(8,128)(2,1)}, bf16[256,768]{1,0:T(8,128)(2,1)}, bf16[2,2,2,64,1024]{4,3,2,1,0:T(8,128)(2,1)}, f32[3,8,256]{2,1,0:T(8,128)}) custom-call(s32[16,280]{1,0:T(8,128)} %mask_ref.1, s32[16]{0:T(128)} %turn_ref.1, s32[2,16]{1,0:T(2,128)} %bitcast.1, bf16[4480,256]{1,0:T(8,128)(2,1)} %tok_hbm.1, ...), custom_call_target="tpu_custom_call" | custom-call | tf_op jit(solution)/shard_map/pallas_call | solution.py:1327
  100.3 5.6 %shard_map.259 = (bf16[1,4480,256]{2,1,0:T(8,128)(2,1)}, bf16[1,4480,256]{2,1,0:T(8,128)(2,1)}, f32[1,256,768]{2,1,0:T(8,128)}, f32[2,256,256]{2,1,0:T(8,128)}, ...) custom-call(bf16[1,4480,256]{2,1,0:T(8,128)(2,1)} %get-tuple-element, ...), custom_call_target="tpu_custom_call" | custom-call | tf_op jit(solution)/shard_map/pallas_call | solution.py:1337

commit v2 on v1

--- a/solution.py
+++ b/solution.py
@@ -655,8 +655,8 @@
             nat_ref[0, 2 * pair + n] = jnp.concatenate([one, jnp.zeros((8, 256), F32)], axis=0).astype(BF16)
 
     def late_start():
-        head_of_row = lax.broadcasted_iota(jnp.int32, (256, 1024), 0) // HEAD
-        head_of_lane = lane_ids((256, 1024)) // 128
+        head_of_row = lax.broadcasted_iota(jnp.int32, (128, 512), 0) // HEAD
+        head_of_lane = lane_ids((128, 512)) // 128
         ones_ref[...] = jnp.where(head_of_row == head_of_lane, 1.0, 0.0).astype(BF16)
         diag_ref[...] = jnp.zeros_like(diag_ref)
         gs_ref[...] = jnp.zeros_like(gs_ref)
@@ -705,7 +705,7 @@
 
     def cross(kind, i):
         low = give_ref[kind, lax.div(i, 2), pl.ds(pl.multiple_of(lax.rem(i, 2) * PAD, 16), PAD)]
-        nat_ref[0, i] = dot_nn(permt_ref[spacing(i)], low).astype(BF16)
+        nat_ref[0, i] = dot_nn(permt_ref[spacing(i)], low).astype(BF16) if kind == 1 else low
         cross_copy(i).start()
 
     def await_cross(i):
@@ -771,6 +771,7 @@
             inverse.append(jnp.where(lane_ids((HALF, 128)) % HEAD < 16, inverses[0], inverses[1]))
         att_ref[i] = join_halves(*attended).astype(BF16)
         inverse_ref[i] = join_halves(*inverse)
+        yield True
         y = (x + dot_nn(att_ref[i], proj_ref[...]) + small_ref[0, 2:3]).astype(BF16)
         record(0, i, y)
         yield True
@@ -801,8 +802,8 @@
         second_mean = jnp.mean(e * xhat, axis=-1, keepdims=True)
         return (g + (e - first_mean - xhat * second_mean) * rstd_ref[t, i]).astype(BF16)
 
-    def feed_backward(i):
-        g = dot_nn(perm_ref[spacing(i)], nat_ref[1 - block, i])
+    def feed_backward(i, natural):
+        g = dot_nn(perm_ref[spacing(i)], natural)
         low = g.astype(BF16)
         nat_ref[1, i] = low
         for part in range(3):
@@ -843,14 +844,15 @@
             query_t = query_all[rows_half].astype(BF16).T
             datt_t = datt.T
             dprob = dot_nt(mask_heads(datt), qkv_ref[i, key_rows, 512:768])
-            totals = dot_nn((datt32 * attended[rows_half]).astype(BF16), ones_ref[...])
+            products = (datt32 * attended[rows_half]).astype(BF16)
+            totals = [dot_nn(products[:, part * 128 : part * 128 + 128], ones_ref[...]) for part in range(2)]
             dkeys = []
             dvalues = []
             ds = []
             for h in range(HEADS):
                 rows = pl.ds(h * HALF, HALF)
                 prob = prob_ref[i, half, rows]
-                total = totals[:, h * 128 : h * 128 + 128]
+                total = totals[h // 4][:, (h % 4) * 128 : (h % 4) * 128 + 128]
                 part = dprob[h * HALF : (h + 1) * HALF]
                 left = prob[:, 0:128].astype(F32) * (part[:, 0:128] - total)
                 right = prob[:, 128:256].astype(F32) * (part[:, 128:256] - total)
@@ -893,26 +895,30 @@
         normed = (xhat * small_ref[t, 0:1] + small_ref[t, 1:2]).astype(BF16)
         wide_acc[t] += dot_tn(normed, dmix)
 
-    def add_feed(at, count):
+    def add_outer(at, count):
         rows = count * PAD
         up = nat_ref[1, pl.ds(at, count)].reshape(rows, 256)
         for part in range(3):
             cols = slice(part * 256, part * 256 + 256)
             slim_acc[0, :, cols] += dot_tn(act_ref[pl.ds(at, count), :, cols].reshape(rows, 256), up)
-        add_in(1, at, count)
         after = up_ref[pl.ds(at, count)].reshape(rows, 256)
         slim_acc[0, :, 768:1024] += dot_tn(att_ref[pl.ds(at, count)].reshape(rows, 256), after)
+
+    def add_feed(at, count):
+        add_outer(at, count)
+        add_in(1, at, count)
 
     def start_feed():
         slim.start_core(0)
         wide.start_core(0)
 
     def backward(i):
-        yield from feed_backward(i)
+        yield from feed_backward(i, nat_ref[0, i])
         yield from attention_backward(i)
 
     def feed_and_sums(i):
-        yield from feed_backward(i)
+        other = jnp.maximum(dil_ref[1, first + i] - 1, 0)
+        yield from feed_backward(i, dot_nn(permt_ref[other], nat_ref[1, i]).astype(BF16))
         yield True
         add_feed(i, 1)
 
@@ -983,11 +989,14 @@
     def _():
         together(backward(images - 1))
         cross(2, images - 1)
-        over(0, images // 4, lambda n: add_feed(4 * n, 4))
-        start_feed()
+        over(0, images // 4, lambda n: add_outer(4 * n, 4))
+        slim.start_core(0)
+        over(0, images // 4, lambda n: add_in(1, 4 * n, 4))
+        wide.start_core(0)
+        slim.start_side(0)
         over(0, images // 4, lambda n: add_in(0, 4 * n, 4))
-        early_sides()
         tall.start_core()
+        wide.start_side(0)
         deliver_all(3, 0)
         slim.start_cut(0)
         deliver_all(0, 0)
@@ -1062,20 +1071,6 @@
         land = land_down.at[1, core]
         return mesh_copy(land, land, far_send, far_recv, across, me)
 
-    side_share(block).wait_recv()
-    share_copy(block).start()
-    pl.when(block == 1)(lambda: cross_share().start())
-    await_bytes(note_all.at[pl.ds(0, dp // 2 - 1)], note_sems.at[5])
-
-    def add_note(j, total):
-        return total + note_all[j]
-
-    notes = lax.fori_loop(0, dp // 2, add_note, jnp.zeros((16, 256), F32))
-    notes_ref[0] = notes[0:8]
-    note_far[0] = notes[8:16]
-    far_copy = mesh_copy(note_far.at[0], note_far.at[1], note_sems.at[6], note_sems.at[7], across, me)
-    far_copy.start()
-
     def in_copies():
         copies = []
         for c in range(2):
@@ -1088,6 +1083,20 @@
         await_bytes(land_in.at[0:128], land_sems.at[0, 1])
         for copy in in_copies():
             copy.start()
+
+    side_share(block).wait_recv()
+    share_copy(block).start()
+    pl.when(block == 1)(lambda: cross_share().start())
+    await_bytes(note_all.at[pl.ds(0, dp // 2 - 1)], note_sems.at[5])
+
+    def add_note(j, total):
+        return total + note_all[j]
+
+    notes = lax.fori_loop(0, dp // 2, add_note, jnp.zeros((16, 256), F32))
+    notes_ref[0] = notes[0:8]
+    note_far[0] = notes[8:16]
+    far_copy = mesh_copy(note_far.at[0], note_far.at[1], note_sems.at[6], note_sems.at[7], across, me)
+    far_copy.start()
 
     @pl.when(block == 1)
     def _():
@@ -1282,7 +1291,7 @@
         pltpu.VMEM((images, PAD, 768), BF16),
         pltpu.VMEM((images, PAD, 256), BF16),
         pltpu.VMEM((images, PAD, 128), F32),
-        pltpu.VMEM((256, 1024), BF16),
+        pltpu.VMEM((128, 512), BF16),
         pltpu.VMEM((2, HALF, 256), F32),
         pltpu.VMEM((16, 2, 2, HALF, 128), F32),
         pltpu.VMEM((8, 256), F32),

time: 106 us -> 104 us (0.981)
  Pallas kernels: 105 us -> 103 us
    pallas_call x1, Pallas kernels: 99.7 us -> 97.2 us  [run_kernels(): pl.pallas_call(functools.partial(section_kernel, images, dp), out_shape=r...]
where the time goes in v2:
time: 104 us
  Pallas kernels  103 us (99%)
    pallas_call x1, Pallas kernels, run_kernels(): pl.pallas_call(functools.partial(section_kernel, images, dp), out_shape=r...  97.2 us
    pallas_call x1, Pallas kernels, run_kernels(): pl.pallas_call(result_kernel, out_shape=out_shape, in_specs=[hbm] * 5, ou...  5.61 us

profile of v2, /device:TPU:1, one launch (start us, length us, event | category | flops | bytes accessed | tf_op | source)
XLA Modules:
  0.0 103.7 jit_solution(14325745222265422986)
XLA Ops:
  0.6 97.2 %shard_map.258 = (bf16[1,4480,256]{2,1,0:T(8,128)(2,1)}, bf16[1,4480,256]{2,1,0:T(8,128)(2,1)}, bf16[256,768]{1,0:T(8,128)(2,1)}, bf16[2,2,2,64,1024]{4,3,2,1,0:T(8,128)(2,1)}, f32[3,8,256]{2,1,0:T(8,128)}) custom-call(s32[16,280]{1,0:T(8,128)} %mask_ref.1, s32[16]{0:T(128)} %turn_ref.1, s32[2,16]{1,0:T(2,128)} %bitcast.1, bf16[4480,256]{1,0:T(8,128)(2,1)} %tok_hbm.1, ...), custom_call_target="tpu_custom_call" | custom-call | tf_op jit(solution)/shard_map/pallas_call | solution.py:1336
  97.9 5.6 %shard_map.259 = (bf16[1,4480,256]{2,1,0:T(8,128)(2,1)}, bf16[1,4480,256]{2,1,0:T(8,128)(2,1)}, f32[1,256,768]{2,1,0:T(8,128)}, f32[2,256,256]{2,1,0:T(8,128)}, ...) custom-call(bf16[1,4480,256]{2,1,0:T(8,128)(2,1)} %get-tuple-element, ...), custom_call_target="tpu_custom_call" | custom-call | tf_op jit(solution)/shard_map/pallas_call | solution.py:1346
